TPU v7x, 512 devices: a whole 4x8x8 slice. The times are simulated.
512 devices in a mesh: row: 16 (over y, core), col: 32 (over x, z).
Axes of the slice: x: 4, y: 8, z: 8, core: 2. Of those that a mesh axis runs over, the one named last changes fastest.
Arguments:
- a_trail: bfloat16 [16384, 16384], P('row', 'col'), may hold values from -6 to 6
- a_panel: bfloat16 [16384, 512], P('row', 'col'), may hold values from -60 to 60
- l_panel: bfloat16 [16384, 512], P('row', 'col'), may hold values from -0.25 to 0.25
- a_diag: bfloat16 [512, 512], P('row'), may hold values from -6 to 6
- linv_diag: bfloat16 [512, 512], P('row'), as said below
Outputs:
- c_trail: bfloat16 [16384, 16384], P('row', 'col')
- c_panel: bfloat16 [16384, 512], P('row', 'col')
- c_diag: bfloat16 [512, 512], P('row', 'col')
- r_band: float32 [256, 256], P('row', 'col')
- q_block: float32 [16384, 256], P('row', 'col')
Inputs may be any that keep to these rules, and one draw needn't show every extreme that they name: linv_diag is lower triangular with diagonal entries between 0.5 and 2.
All inputs are finite; a program needn't handle non-finite values.
Results may differ from a plain program's by a relative error of at most 0.015.
Values may be sent and summed in bfloat16 or wider, within the bound.
No kernel may reach another device: no remote copies, remote signals or barrier semaphores. Data moves between devices by JAX's collectives and lax.ppermute only.
A program may use at most 64 MiB of HBM per device.

v0:
```python
import jax
import jax.numpy as jnp
from jax import lax
from jax.sharding import PartitionSpec as P

BW = 256


def broadcast(block, axis, owner):
    block = jnp.where(lax.axis_index(axis) == owner, block, jnp.zeros_like(block))
    return lax.psum(block, axis)


def rows_against(left, right):
    return jnp.einsum("ik,jk->ij", left, right, preferred_element_type=jnp.float32)


def body(a_trail, a_panel, l_panel, a_diag, linv_diag):
    row_count = lax.axis_size("row")
    col_count = lax.axis_size("col")
    row_index = lax.axis_index("row")
    col_index = lax.axis_index("col")
    diag_full, linv_full = (
        lax.all_gather(a_diag, "row", axis=0, tiled=True),
        lax.all_gather(linv_diag, "row", axis=0, tiled=True),
    )
    inner = jnp.dot(linv_full, diag_full, preferred_element_type=jnp.float32).astype(jnp.bfloat16)
    congruent = rows_against(inner, linv_full).astype(jnp.bfloat16)
    a_rows, l_rows = (
        lax.all_gather(a_panel, "col", axis=1, tiled=True),
        lax.all_gather(l_panel, "col", axis=1, tiled=True),
    )
    half_term = 0.5 * jnp.dot(l_rows, congruent, preferred_element_type=jnp.float32)
    first_pass = (rows_against(a_rows, linv_full) - half_term).astype(jnp.bfloat16)
    col_width = a_trail.shape[1]
    ratio = col_count // row_count
    owner = col_index // ratio
    offset = col_index % ratio * col_width
    both = jnp.stack((first_pass, l_rows))
    owner_rows = broadcast(both, "row", owner)
    matched = lax.dynamic_slice_in_dim(owner_rows, offset, col_width, 1)
    update = rows_against(first_pass, matched[1]) + rows_against(l_rows, matched[0])
    c_trail = (a_trail.astype(jnp.float32) - update).astype(jnp.bfloat16)
    finished = (first_pass.astype(jnp.float32) - half_term).astype(jnp.bfloat16)
    panel_width = a_panel.shape[1]
    c_panel = lax.dynamic_slice_in_dim(finished, col_index * panel_width, panel_width, 1)
    diag_rows = a_diag.shape[0]
    block_order = a_diag.shape[1]
    diag_cols = block_order // col_count
    c_diag = lax.dynamic_slice(
        congruent, (row_index * diag_rows, col_index * diag_cols), (diag_rows, diag_cols)
    )
    band = BW
    order = a_trail.shape[0] * row_count
    panel_bits = finished[:, :band]
    column_block = panel_bits.astype(jnp.float32)
    local_gram = jnp.einsum("ki,kj->ij", panel_bits, panel_bits, preferred_element_type=jnp.float32)
    local_factor = jnp.linalg.cholesky(local_gram)
    stacked = lax.all_gather(
        local_factor[None].astype(jnp.bfloat16), "row", axis=0, tiled=True
    ).astype(jnp.float32)
    gram = jnp.einsum("rik,rjk->ij", stacked, stacked, precision=lax.Precision.HIGHEST)
    lower = jnp.linalg.cholesky(gram * (1.0 / order))
    upper = lower.T
    band_rows = band // row_count
    band_cols = band // col_count
    r_band = lax.dynamic_slice(
        upper, (row_index * band_rows, col_index * band_cols), (band_rows, band_cols)
    )
    q_rows = jax.scipy.linalg.solve_triangular(lower, column_block.T, lower=True).T
    q_block = lax.dynamic_slice_in_dim(q_rows, col_index * band_cols, band_cols, 1)
    return (c_trail, c_panel, c_diag, r_band, q_block)


def solution(mesh):
    return jax.shard_map(
        body,
        mesh=mesh,
        in_specs=(
            P("row", "col"),
            P("row", "col"),
            P("row", "col"),
            P("row", None),
            P("row", None),
        ),
        out_specs=(
            P("row", "col"),
            P("row", "col"),
            P("row", "col"),
            P("row", "col"),
            P("row", "col"),
        ),
        check_vma=False,
    )
```

profile of v0, /device:TPU:1, one launch (start us, length us, event | category | flops | bytes accessed | tf_op | source)
XLA Modules:
  0.0 434.2 jit_solution(6111433595781809176)
XLA Ops:
  7.2 0.7 all-gather.7.cloned.1.call-update
  7.9 0.7 all-gather.5.cloned.1.call-update
  8.7 22.7 %all_gather.16 = bf16[512,512]{1,0:T(8,128)(2,1)S(1)} all-gather(bf16[32,512]{1,0:T(8,128)(2,1)} %param.10), channel_id=1, replica_groups=mesh['row'=16,'col'=32] {'row'}, dimensions={0}, use_global_device_ids=true | all-gather | bytes 557056 | tf_op jit(solution)/shard_map/all_gather | solution.py:25
  31.4 17.6 %all_gather.17 = bf16[512,512]{1,0:T(8,128)(2,1)S(1)} all-gather(bf16[32,512]{1,0:T(8,128)(2,1)} %param.9), channel_id=1, replica_groups=mesh['row'=16,'col'=32] {'row'}, dimensions={0}, use_global_device_ids=true | all-gather | bytes 557056 | tf_op jit(solution)/shard_map/all_gather | solution.py:24
  49.0 0.8 convolution_convert_fusion
  49.8 44.6 %all-gather.7.cloned.1.call-done = bf16[1024,512]{0,1:T(8,128)(2,1)} async-done(((bf16[1024,16]{0,1:T(8,128)(2,1)}), bf16[1024,512]{0,1:T(8,128)(2,1)}) %all-gather.7.cloned.1.call-update) | async-done | bytes 1048592 | tf_op jit(solution)/shard_map/all_gather | solution.py:31
  94.5 1.9 fusion.32
  96.4 80.7 %all-gather.5.cloned.1.call-done = bf16[1024,512]{0,1:T(8,128)(2,1)} async-done(((bf16[1024,16]{0,1:T(8,128)(2,1)}), bf16[1024,512]{0,1:T(8,128)(2,1)}) %all-gather.5.cloned.1.call-update) | async-done | bytes 1048592 | tf_op jit(solution)/shard_map/all_gather | solution.py:30
  177.1 2.1 fusion.3
  179.3 1.0 copy-done.1
  180.8 11.7 %cholesky.130 = f32[128,128]{1,0:T(8,128)S(1)} custom-call(f32[128,128]{1,0:T(8,128)S(1)} %cholesky.194), custom_call_target="Cholesky" | custom-call | tf_op jit(solution)/shard_map/jit(cholesky)/cholesky | solution.py:58
  192.5 1.5 maximum_select_fusion
  194.4 10.4 %custom-call.14 = f32[1,128,128]{1,2,0:T(8,128)} custom-call(f32[1,128,128]{2,1,0:T(8,128)S(1)} %get-tuple-element.33), custom_call_target="InvertDiagBlocksLowerTriangular" | custom-call | tf_op jit(solution)/shard_map/jit(cholesky)/cholesky | solution.py:58
  204.8 0.8 cholesky.155
  205.7 1.1 constant_dynamic-update-slice_fusion.1
  206.7 0.9 convolution_subtract_fusion.2
  207.6 12.5 %cholesky.147 = f32[128,128]{1,0:T(8,128)S(1)} custom-call(f32[128,128]{1,0:T(8,128)} %convolution_subtract_fusion.2), custom_call_target="Cholesky" | custom-call | tf_op jit(solution)/shard_map/jit(cholesky)/cholesky | solution.py:58
  222.1 0.7 fusion.14
  222.9 1.4 dynamic_slice.17
  224.9 0.8 slice_bitcast_fusion
  225.7 90.2 %all-reduce.3.cloned.1.call-done = bf16[2,1024,512]{1,2,0:T(8,128)(2,1)} async-done(((bf16[2,1024,512]{1,2,0:T(8,128)(2,1)}), bf16[2,1024,512]{1,2,0:T(8,128)(2,1)}) %all-reduce.3.cloned.1.call-update) | async-done | bytes 2097168 | tf_op jit(solution)/shard_map/psum | solution.py:11
  316.0 1.8 fusion.5
  317.7 2.8 fusion.1
  320.6 40.6 %all-gather.9.cloned.1.call-done = bf16[4096,256]{1,0:T(8,128)(2,1)} async-done(((bf16[256,256]{1,0:T(8,128)(2,1)}), bf16[4096,256]{1,0:T(8,128)(2,1)}) %all-gather.9.cloned.1.call-update) | async-done | bytes 2097168 | tf_op jit(solution)/shard_map/all_gather | solution.py:59
  361.2 3.0 fusion.4
  364.4 11.9 %cholesky.164 = f32[128,128]{1,0:T(8,128)S(1)} custom-call(f32[128,128]{1,0:T(8,128)S(1)} %cholesky.197), custom_call_target="Cholesky" | custom-call | tf_op jit(solution)/shard_map/jit(cholesky)/cholesky | solution.py:63
  376.9 9.8 %custom-call.15 = f32[1,128,128]{1,2,0:T(8,128)S(1)} custom-call(f32[1,128,128]{2,1,0:T(8,128)S(1)} %get-tuple-element.29), custom_call_target="InvertDiagBlocksLowerTriangular" | custom-call | tf_op jit(solution)/shard_map/jit(cholesky)/cholesky | solution.py:63
  387.2 11.7 %cholesky.181 = f32[128,128]{1,0:T(8,128)S(1)} custom-call(f32[128,128]{1,0:T(8,128)S(1)} %convolution_subtract_fusion.1), custom_call_target="Cholesky" | custom-call | tf_op jit(solution)/shard_map/jit(cholesky)/cholesky | solution.py:63
  401.0 3.9 while.1
  401.6 1.4 bitcast_dynamic-update-slice_fusion.2
  403.6 1.4 bitcast_dynamic-update-slice_fusion.2
  405.0 19.7 %custom-call.12 = f32[2,128,128]{1,2,0:T(8,128)S(1)} custom-call(f32[2,128,128]{2,1,0:T(8,128)S(1)} %get-tuple-element.13), custom_call_target="InvertDiagBlocksLowerTriangular" | custom-call | tf_op jit(solution)/shard_map/jit(_solve_triangular)/triangular_solve | solution.py:70
  (52 shorter events, 8.5 us)
Async XLA Ops:
  7.2 87.3 %all-gather.7.cloned.1.call-start = ((), (), s32[]{:S(2)}) async-start(), calls=%async_computation.1 | async-start | bytes 1081344 | tf_op jit(solution)/shard_map/all_gather | solution.py:31
  7.9 169.2 %all-gather.5.cloned.1.call-start = ((), (), s32[]{:S(2)}) async-start(), calls=%async_computation | async-start | bytes 1081344 | tf_op jit(solution)/shard_map/all_gather | solution.py:30
  8.6 307.3 %all-reduce.3.cloned.1.call-start = ((), (), s32[]{:S(2)}) async-start(), calls=%async_computation.2 | async-start | bytes 4194304 | tf_op jit(solution)/shard_map/psum | solution.py:11
  31.4 65.0 %copy-start.4 = (bf16[512,512]{1,0:T(8,128)(2,1)}, bf16[512,512]{1,0:T(8,128)(2,1)S(1)}, u32[]{:S(2)}) copy-start(bf16[512,512]{1,0:T(8,128)(2,1)S(1)} %all_gather.16) | copy-start | bytes 1572868
  49.8 46.6 %copy-start.6 = (bf16[512,512]{0,1:T(8,128)(2,1)}, bf16[512,512]{0,1:T(8,128)(2,1)S(1)}, u32[]{:S(2)}) copy-start(bf16[512,512]{0,1:T(8,128)(2,1)S(1)} %convolution_convert_fusion) | copy-start | bytes 1572868
  179.3 1.0 copy-start.1
  179.3 13.2 %copy-start = (bf16[1024,512]{0,1:T(8,128)(2,1)S(1)}, bf16[1024,512]{0,1:T(8,128)(2,1)}, u32[]{:S(2)}) copy-start(bf16[1024,512]{0,1:T(8,128)(2,1)} %all-gather.7.cloned.1.call-done) | copy-start | bytes 3145732
  192.5 1.8 copy-start.7
  194.1 30.2 %copy-start.2 = (bf16[1024,512]{0,1:T(8,128)(2,1)S(1)}, bf16[1024,512]{0,1:T(8,128)(2,1)}, u32[]{:S(2)}) copy-start(bf16[1024,512]{0,1:T(8,128)(2,1)} %copy-done.1) | copy-start | bytes 3145732
  194.1 167.1 %all-gather.9.cloned.1.call-start = ((), (), s32[]{:S(2)}) async-start(), calls=%async_computation.3 | async-start | bytes 2228224 | tf_op jit(solution)/shard_map/all_gather | solution.py:59
  225.7 92.0 %copy-start.5 = (bf16[1024,512]{1,0:T(8,128)(2,1)S(1)}, bf16[1024,512]{1,0:T(8,128)(2,1)}, u32[]{:S(2)}) copy-start(bf16[1024,512]{1,0:T(8,128)(2,1)} %param.6) | copy-start | bytes 3145732
  364.2 60.5 %copy-start.3 = (bf16[256,1024]{1,0:T(8,128)(2,1)S(1)}, bf16[256,1024]{1,0:T(8,128)(2,1)}, u32[]{:S(2)}) copy-start(bf16[256,1024]{1,0:T(8,128)(2,1)} %slice_bitcast_fusion) | copy-start | bytes 1572868
Sparse Core Ops, SparseCore 0:
  11.2 83.2 all-gather.6
  97.6 79.4 all-gather.4
  194.2 121.6 all-reduce.2
  317.9 43.2 all-gather.8
where the time goes:
time: 435 us; the launch traced here: 434 us
  waiting for transfers between devices  258 us (59%)
  other arithmetic  92.8 us (21%)
  blocking collectives  40.3 us (9%)
  matrix products  16.9 us (4%)
  between operations  16.7 us (4%)
  local copies, waits for them, and re-layouts  9.57 us (2%)
    psum x1, waiting for transfers between devices, broadcast(): return lax.psum(block, axis)  90.2 us
    all_gather x1, waiting for transfers between devices, body(): lax.all_gather(a_panel, 'col', axis=1, tiled=True)  80.7 us
    all_gather x1, waiting for transfers between devices, body(): lax.all_gather(l_panel, 'col', axis=1, tiled=True)  44.6 us
    all_gather x1, waiting for transfers between devices, body(): lax.all_gather(local_factor[None].astype(jnp.bfloat16), 'row', axis=0, ti...  40.6 us
    another operation x6, other arithmetic, body(): local_factor = jnp.linalg.cholesky(local_gram)  35.4 us
    another operation x7, other arithmetic, body(): lower = jnp.linalg.cholesky(gram * (1.0 / order))  34.7 us
    all_gather x1, blocking collectives, body(): lax.all_gather(linv_diag, 'row', axis=0, tiled=True)  22.7 us
    another operation x3, other arithmetic, body(): jax.scipy.linalg.solve_triangular(lower, column_block.T, lower=True)  19.7 us
  transfers between devices with their start and end apart: 4, of which 4 were waited for; matrix products, arithmetic and copies ran while one was open for 9% of the time, Pallas kernels for 0%

commit v1 on v0

v1 whole, which is shorter than its diff:
```python
import functools

import jax
import jax.numpy as jnp
from jax import lax
from jax.experimental import pallas as pl
from jax.experimental.pallas import tpu as pltpu
from jax.sharding import PartitionSpec as P

BW = 256
PANEL = 16
X_COUNT, Z_COUNT = 4, 8
VMEM_LIMIT = 48 * 1024 * 1024

f32, bf16 = jnp.float32, jnp.bfloat16


def dot(left, right, left_dim, right_dim):
    return lax.dot_general(
        left, right, (((left_dim,), (right_dim,)), ((), ())), preferred_element_type=f32
    )


def spread(block, axis, count, groups=None):
    return lax.all_to_all(
        jnp.broadcast_to(block[None], (count,) + block.shape), axis, 0, 0, axis_index_groups=groups
    )


def panel_kernel(diag, rows, first, panel, panel_cols, congruent, gram):
    order = diag.shape[3]
    a_diag = diag[:, 0].reshape(order, order)
    linv = diag[:, 1].reshape(order, order)
    width = rows.shape[3]
    a_rows = rows[:, 0].reshape(order, width)
    l_rows = rows[:, 1].reshape(order, width)
    inner = dot(linv, a_diag, 1, 0).astype(bf16)
    c = dot(inner, linv, 1, 1).astype(bf16)
    congruent[...] = c
    half = 0.5 * dot(c, l_rows, 0, 0)
    f = (dot(linv, a_rows, 1, 0) - half).astype(bf16)
    first[...] = f
    p = (f.astype(f32) - half).astype(bf16)
    panel[...] = p
    own = panel_cols.shape[0]
    start = pl.multiple_of(lax.axis_index("col") * own, own)
    panel_cols[...] = panel[pl.ds(start, own), :]
    band = gram.shape[0]
    gram[...] = dot(p[:band], p[:band], 1, 1)


def split(x):
    high = x.astype(bf16)
    rest = x - high.astype(f32)
    middle = rest.astype(bf16)
    low = (rest - middle.astype(f32)).astype(bf16)
    return high, middle, low


def factor_kernel(scale, gram, panel, r_rows, q_cols, g, w):
    band = g.shape[0]
    g[...] = gram[...].reshape(band, band) * scale
    row_id = lax.broadcasted_iota(jnp.int32, (band, band), 0)
    col_id = lax.broadcasted_iota(jnp.int32, (band, band), 1)
    w[...] = jnp.where(row_id == col_id, 1.0, 0.0)
    sub = lax.broadcasted_iota(jnp.int32, (PANEL, 128), 0)
    for s in range(0, band, PANEL):
        left = s // 128 * 128
        right = (s // 128 + 1) * 128
        rows = pl.ds(s, PANEL)
        parts = [g[rows, pl.ds(o, 128)] for o in range(left, band, 128)]
        n_g = len(parts)
        parts += [w[rows, pl.ds(o, 128)] for o in range(0, right, 128)]
        cols = [
            jnp.broadcast_to(parts[0][:, s - left + t : s - left + t + 1], (PANEL, 128))
            for t in range(PANEL)
        ]
        pivots = jnp.zeros((PANEL, 128), f32)
        for j in range(PANEL):
            pivot = cols[j][j : j + 1, :]
            pivots = jnp.where(sub == j, pivot, pivots)
            if j == PANEL - 1:
                break
            m = jnp.where(sub > j, cols[j] * (1.0 / pivot), 0.0)
            for t in range(j + 1, PANEL):
                cols[t] = cols[t] - m * cols[t][j : j + 1, :]
            parts = [part - m * part[j : j + 1, :] for part in parts]
        root = lax.rsqrt(pivots)
        parts = [part * root for part in parts]
        for i, o in enumerate(range(left, band, 128)):
            g[rows, pl.ds(o, 128)] = parts[i]
        for i, o in enumerate(range(0, right, 128)):
            w[rows, pl.ds(o, 128)] = parts[n_g + i]
        done = s + PANEL
        if done == band:
            break
        top = done // 128 * 128
        u = jnp.concatenate(parts, axis=1)
        h, m, l = split(u)
        a = top - left
        b = band - left
        lefts = jnp.concatenate([x[:, a:b] for x in (h, h, m, h, m, l)], axis=0)
        rights = jnp.concatenate([h, m, h, l, m, h], axis=0)
        update = dot(lefts, rights, 0, 0)[done - top :]
        rest = pl.ds(done, band - done)
        g[rest, pl.ds(left, band - left)] = g[rest, pl.ds(left, band - left)] - update[:, :b]
        w[rest, pl.ds(0, right)] = w[rest, pl.ds(0, right)] - update[:, b:]
    count = q_cols.shape[0]
    start = pl.multiple_of(lax.axis_index("col") * count, count)
    inverse = jnp.concatenate(list(split(w[pl.ds(start, count), :])), axis=0)
    q = dot(inverse, panel[...], 1, 0)
    q_cols[...] = q[:count] + q[count : 2 * count] + q[2 * count :]
    own = r_rows.shape[0]
    start = pl.multiple_of(lax.axis_index("row") * own, own)
    column = lax.broadcasted_iota(jnp.int32, (own, band), 1)
    row = lax.broadcasted_iota(jnp.int32, (own, band), 0) + start
    r_rows[...] = jnp.where(column >= row, g[pl.ds(start, own), :], 0.0)


def trail_kernel(diag, congruent, rows, first, cols, a_trail, c_trail):
    order = diag.shape[3]
    linv = diag[:, 1].reshape(order, order)
    width = cols.shape[3]
    a_cols = cols[:, 0].reshape(order, width)
    l_cols = cols[:, 1].reshape(order, width)
    half = 0.5 * dot(congruent[...], l_cols, 0, 0)
    first_cols = (dot(linv, a_cols, 1, 0) - half).astype(bf16)
    l_rows = rows[:, 1].reshape(order, rows.shape[3])
    update = dot(first[...], l_cols, 0, 0) + dot(l_rows, first_cols, 0, 0)
    c_trail[...] = (a_trail[...].astype(f32) - update).astype(bf16)


def call(kernel, outs, *operands, scratch=()):
    return pl.pallas_call(
        kernel,
        out_shape=[jax.ShapeDtypeStruct(shape, dtype) for shape, dtype in outs],
        in_specs=[pl.BlockSpec(memory_space=pltpu.VMEM)] * len(operands),
        out_specs=[pl.BlockSpec(memory_space=pltpu.VMEM)] * len(outs),
        scratch_shapes=list(scratch),
        compiler_params=pltpu.CompilerParams(vmem_limit_bytes=VMEM_LIMIT),
    )(*operands)


def body(a_trail, a_panel, l_panel, a_diag, linv_diag):
    row_count = lax.axis_size("row")
    col_count = lax.axis_size("col")
    row_index = lax.axis_index("row")
    col_index = lax.axis_index("col")
    x_index, z_index = col_index // Z_COUNT, col_index % Z_COUNT
    z_groups = [[x * Z_COUNT + z for z in range(Z_COUNT)] for x in range(X_COUNT)]
    x_groups = [[x * Z_COUNT + z for x in range(X_COUNT)] for z in range(Z_COUNT)]
    height, own = a_panel.shape
    order = a_diag.shape[1]
    width = a_trail.shape[1]

    diag = lax.all_gather(jnp.stack((a_diag, linv_diag)), "row", axis=0)

    pair = jnp.stack((a_panel.T, l_panel.T))
    by_z = spread(pair, "col", Z_COUNT, z_groups)
    rows = spread(by_z, "col", X_COUNT, x_groups).reshape(col_count, 2, own, height)

    halves = height // width
    piece = Z_COUNT // (Z_COUNT // halves)
    per = Z_COUNT // halves
    half_index, quarter = z_index // per, z_index % per
    share = lax.dynamic_slice(
        by_z, (quarter * piece, 0, 0, half_index * width), (piece, 2, own, width)
    )
    moves = []
    for r in range(row_count):
        for c in range(col_count):
            x, z = c // Z_COUNT, c % Z_COUNT
            target = (x * per + z % per) * col_count + r * halves + z // per
            moves.append((r * col_count + c, target))
    share = lax.ppermute(share, ("row", "col"), moves)
    cols = lax.all_gather(share, "row", axis=0).reshape(col_count, 2, own, width)

    first, panel, panel_cols, congruent, gram = call(
        panel_kernel,
        [
            ((order, height), bf16),
            ((order, height), bf16),
            ((own, height), bf16),
            ((order, order), bf16),
            ((BW, BW), f32),
        ],
        diag,
        rows,
    )
    parts = lax.all_to_all(gram.reshape(row_count, BW // row_count, BW), "row", 0, 0)
    gram = spread(parts.sum(axis=0), "row", row_count)
    r_rows, q_cols = call(
        functools.partial(factor_kernel, 1.0 / (height * row_count)),
        [((BW // row_count, BW), f32), ((BW // col_count, height), f32)],
        gram,
        panel[:BW],
        scratch=[pltpu.VMEM((BW, BW), f32), pltpu.VMEM((BW, BW), f32)],
    )
    (c_trail,) = call(
        trail_kernel,
        [(a_trail.shape, bf16)],
        diag,
        congruent,
        rows,
        first,
        cols,
        a_trail,
    )
    band_cols = BW // col_count
    r_band = lax.dynamic_slice_in_dim(r_rows, col_index * band_cols, band_cols, 1)
    diag_rows = a_diag.shape[0]
    c_diag = lax.dynamic_slice(
        congruent, (row_index * diag_rows, col_index * own), (diag_rows, own)
    )
    return (c_trail, panel_cols.T, c_diag, r_band, q_cols.T)


def solution(mesh):
    both = P("row", "col")
    return jax.shard_map(
        body,
        mesh=mesh,
        in_specs=(both, both, both, P("row", None), P("row", None)),
        out_specs=(both, both, both, both, both),
        check_vma=False,
    )
```

time: 435 us -> 132 us (0.30)
  waiting for transfers between devices: 258 us -> 18.7 us
  other arithmetic: 92.8 us -> 2.22 us
  matrix products: 16.9 us -> 0 us
  Pallas kernels: 0 us -> 15.5 us
  blocking collectives: 40.3 us -> 52.6 us
  starting transfers between devices: 0.34 us -> 11.9 us
  local copies, waits for them, and re-layouts: 9.57 us -> 15.7 us
    all_gather x3 -> x2, waiting for transfers between devices: 166 us -> 10.1 us  [the longest x1 10.1 us: body(): diag = lax.all_gather(jnp.stack((a_diag, linv_diag)), 'row', axis=0)]
    psum x1 -> x0, waiting for transfers between devices: 90.2 us -> none  [broadcast(): return lax.psum(block, axis)]
    another operation x16 -> x2, other arithmetic: 89.8 us -> 2.2 us  [the longest x1 1.41 us: body(): diag = lax.all_gather(jnp.stack((a_diag, linv_diag)), 'row', axis=0)]
    all_to_all x0 -> x2, blocking collectives: none -> 52.6 us  [the longest x1 26.6 us: spread(): lax.all_to_all(jnp.broadcast_to(block[None], (count,) + block.shape), axi...]
    all_gather x2 -> x0, blocking collectives: 40.3 us -> none  [the longest x1 22.7 us: body(): lax.all_gather(linv_diag, 'row', axis=0, tiled=True)]
    pallas_call x0 -> x3, Pallas kernels: none -> 15.5 us  [call(): pl.pallas_call(kernel, out_shape=[jax.ShapeDtypeStruct(shape, dtype) for...]
    dot_general x7 -> x0, matrix products: 12.8 us -> none  [the longest x4 7.58 us: rows_against(): jnp.einsum('ik,jk->ij', left, right, preferred_element_type=jnp.float32)]
    unnamed x16 -> x24, local copies, waits for them, and re-layouts: 0.98 us -> 11.4 us
  transfers between devices with their start and end apart: 4 -> 5, of which waited for: 4 -> 3; matrix products, arithmetic and copies ran while one was open for 9% -> 4% of each run, Pallas kernels for 0% -> 6%
where the time goes in v1:
time: 132 us; the launch traced here: 131 us
  blocking collectives  52.6 us (40%)
  waiting for transfers between devices  18.7 us (14%)
  local copies, waits for them, and re-layouts  15.7 us (12%)
  Pallas kernels  15.5 us (12%)
  between operations  14.1 us (11%)
  starting transfers between devices  11.9 us (9%)
  other arithmetic  2.22 us (2%)
    all_to_all x1, blocking collectives, spread(): lax.all_to_all(jnp.broadcast_to(block[None], (count,) + block.shape), axi...  26.6 us
    all_to_all x1, blocking collectives, body(): lax.all_to_all(gram.reshape(row_count, BW // row_count, BW), 'row', 0, 0)  26.1 us
    pallas_call x3, Pallas kernels, call(): pl.pallas_call(kernel, out_shape=[jax.ShapeDtypeStruct(shape, dtype) for...  15.5 us
    unnamed x24, local copies, waits for them, and re-layouts  11.4 us
    all_gather x1, waiting for transfers between devices, body(): diag = lax.all_gather(jnp.stack((a_diag, linv_diag)), 'row', axis=0)  10.1 us
    all_to_all x2, starting transfers between devices, spread(): lax.all_to_all(jnp.broadcast_to(block[None], (count,) + block.shape), axi...  7.52 us
    all_to_all x2, waiting for transfers between devices, spread(): lax.all_to_all(jnp.broadcast_to(block[None], (count,) + block.shape), axi...  5.44 us
    ppermute x1, starting transfers between devices, body(): share = lax.ppermute(share, ('row', 'col'), moves)  4.32 us
  transfers between devices with their start and end apart: 5, of which 3 were waited for; matrix products, arithmetic and copies ran while one was open for 4% of the time, Pallas kernels for 6%

profile of v1, /device:TPU:1, one launch (start us, length us, event | category | flops | bytes accessed | tf_op | source)
XLA Modules:
  0.0 130.7 jit_solution(13765940803232646268)
XLA Ops:
  7.2 0.0 all-gather.5.cloned.1.call-start
  7.2 1.4 %pad_maximum_fusion = bf16[2,32,512]{2,1,0:T(8,128)(2,1)} fusion(bf16[1,32,512]{2,1,0:T(8,128)(2,1)} %bitcast.18, bf16[1,32,512]{2,1,0:T(8,128)(2,1)} %bitcast.19), kind=kLoop, calls=%fused_computation | loop fusion | flops 32768 | bytes 131072 | tf_op jit(solution)/shard_map/stack | solution.py:156
  8.6 0.0 all-gather.5.cloned.1.call-update
  8.6 0.8 pad_maximum_fusion.1
  9.5 26.6 %all_to_all.20 = bf16[8,2,16,1024]{3,2,1,0:T(8,128)(2,1)S(1)} all-to-all(bf16[8,2,16,1024]{3,2,1,0:T(8,128)(2,1)S(1)} %broadcast_in_dim.6), channel_id=1, replica_groups={{0,1,2,3,4,5,6,7},{8,9,10,11,12,13,14,15},{16,17,18,19,20,21,22,23},{24..., dimensions={0} | all-to-all | bytes 1048576 | tf_op jit(solution)/shard_map/all_to_all | solution.py:25
  36.1 1.6 %broadcast_in_dim.7 = bf16[4,8,2,16,1024]{4,3,2,1,0:T(8,128)(2,1)} broadcast(bf16[8,2,16,1024]{3,2,1,0:T(8,128)(2,1)S(1)} %all_to_all.20), dimensions={1,2,3,4} | broadcast | bytes 2621440 | tf_op jit(solution)/shard_map/broadcast_in_dim | solution.py:26
  37.7 4.1 %all-to-all-start.1 = ((bf16[4,8,2,16,1024]{4,3,2,1,0:T(8,128)(2,1)}), bf16[4,8,2,16,1024]{4,3,2,1,0:T(8,128)(2,1)S(1)}, u32[]{:S(2)}, u32[]{:S(2)}) async-start(bf16[4,8,2,16,1024]{4,3,2,1,0:T(8,128)(2,1)} %broadcast_in_dim.7), calls=%async_computation.1 | async-start | bytes 4194304 | tf_op jit(solution)/shard_map/all_to_all | solution.py:25
  41.8 4.3 %collective-permute-start = (bf16[2,2,16,512]{3,2,1,0:T(8,128)(2,1)S(1)}, bf16[2,2,16,512]{3,2,1,0:T(8,128)(2,1)S(1)}, u32[]{:S(2)}, u32[]{:S(2)}) collective-permute-start(bf16[2,2,16,512]{3,2,1,0:T(8,128)(2,1)S(1)} %constant_dynamic-slice_fusion.1), channel_id=1, source_target_pairs={{0,0},{1,32},{2,64},{3,96},{4,1},{5,33},{6,65},{7,97},{8,128},{9,1... | collective-permute-start | bytes 196616 | tf_op jit(solution)/shard_map/ppermute | solution.py:175
  46.1 3.2 %collective-permute-done = bf16[2,2,16,512]{3,2,1,0:T(8,128)(2,1)S(1)} collective-permute-done((bf16[2,2,16,512]{3,2,1,0:T(8,128)(2,1)S(1)}, bf16[2,2,16,512]{3,2,1,0:T(8,128)(2,1)S(1)}, u32[]{:S(2)}, u32[]{:S(2)}) %collective-permute-start) | collective-permute-done | bytes 65568 | tf_op jit(solution)/shard_map/ppermute | solution.py:175
  49.2 0.6 copy-done.10
  49.9 10.1 %all-gather.5.cloned.1.call-done = bf16[32,32,512]{2,1,0:T(8,128)(2,1)} async-done(((bf16[2,32,512]{2,1,0:T(8,128)(2,1)}), bf16[32,32,512]{2,1,0:T(8,128)(2,1)}) %all-gather.5.cloned.1.call-update) | async-done | bytes 1048592 | tf_op jit(solution)/shard_map/all_gather | solution.py:156
  60.0 5.4 %all-to-all-done.1 = bf16[4,8,2,16,1024]{4,3,2,1,0:T(8,128)(2,1)S(1)} async-done(((bf16[4,8,2,16,1024]{4,3,2,1,0:T(8,128)(2,1)}), bf16[4,8,2,16,1024]{4,3,2,1,0:T(8,128)(2,1)S(1)}, u32[]{:S(2)}, u32[]{:S(2)}) %all-to-all-start.1) | async-done | bytes 2097184 | tf_op jit(solution)/shard_map/all_to_all | solution.py:25
  65.4 2.0 %copy-done.1 = bf16[32,32,512]{2,1,0:T(8,128)(2,1)S(1)} copy-done((bf16[32,32,512]{2,1,0:T(8,128)(2,1)S(1)}, bf16[32,32,512]{2,1,0:T(8,128)(2,1)}, u32[]{:S(2)}) %copy-start.1) | copy-done | bytes 1048600
  67.4 2.9 %shard_map.92 = (bf16[512,1024]{1,0:T(8,128)(2,1)S(1)}, bf16[512,1024]{1,0:T(8,128)(2,1)S(1)}, bf16[16,1024]{1,0:T(8,128)(2,1)}, bf16[512,512]{1,0:T(8,128)(2,1)S(1)}, f32[256,256]{1,0:T(8,128)S(1)}) custom-call(bf16[16,2,32,512]{3,2,1,0:T(8,128)(2,1)S(1)} %bitcast.15, bf16[32,2,16,1024]{3,2,1,0:T(8,128)(2,1)S(1)} %bitcast.13), custom_call_target="tpu_custom_call" | custom-call | tf_op jit(solution)/shard_map/pallas_call | solution.py:134
  70.2 1.0 copy-done.5
  71.2 0.8 copy-done.7
  72.0 1.0 copy-done.9
  73.0 26.1 %all_to_all.21 = f32[16,16,256]{2,1,0:T(8,128)S(1)} all-to-all(f32[16,16,256]{2,1,0:T(8,128)S(1)} %bitcast.17), channel_id=1, replica_groups=mesh['row'=16,'col'=32] {'row'}, dimensions={0} | all-to-all | bytes 524288 | tf_op jit(solution)/shard_map/all_to_all | solution.py:190
  99.1 0.7 broadcast_in_dim.8
  99.8 3.4 %all-to-all-start.3 = ((f32[16,16,256]{2,1,0:T(8,128)}), f32[16,16,256]{2,1,0:T(8,128)S(1)}, u32[]{:S(2)}, u32[]{:S(2)}) async-start(f32[16,16,256]{2,1,0:T(8,128)} %broadcast_in_dim.8), calls=%async_computation.3 | async-start | bytes 524288 | tf_op jit(solution)/shard_map/all_to_all | solution.py:25
  103.2 0.8 dynamic_slice.10
  104.0 0.7 copy.12
  104.7 1.1 slice.3.panel
  105.8 0.0 all-gather.7.cloned.1.call-done.cols
  105.8 1.2 copy-done.3
  107.0 1.2 copy-done.4
  108.3 1.2 copy-done.6
  109.5 1.0 copy-done.8
  110.5 4.5 %shard_map.93 = bf16[1024,512]{1,0:T(8,128)(2,1)} custom-call(bf16[16,2,32,512]{3,2,1,0:T(8,128)(2,1)S(1)} %bitcast.16, bf16[512,512]{1,0:T(8,128)(2,1)S(1)} %copy-done.8, bf16[32,2,16,1024]{3,2,1,0:T(8,128)(2,1)} %bitcast.14, bf16[512,1024]{1,0:T(8,128)(2,1)S(1)} %copy-done.6, bf16[32,2,16,512]{3,2,1,0:T(8,128)(2,1)S(1)} %copy-done.4, ...), custom_call_target="tpu_custom_call" | custom-call | tf_op jit(solution)/shard_map/pallas_call | solution.py:134
  115.0 8.1 %shard_map.94 = (f32[16,256]{1,0:T(8,128)S(1)}, f32[8,1024]{1,0:T(8,128)}) custom-call(f32[16,16,256]{2,1,0:T(8,128)S(1)} %all-to-all-done.3.gram, bf16[256,1024]{1,0:T(8,128)(2,1)S(1)} %slice.3.panel), custom_call_target="tpu_custom_call" | custom-call | tf_op jit(solution)/shard_map/pallas_call | solution.py:134
  123.2 0.1 constant_dynamic-slice_fusion
  123.2 0.7 copy.13
  (19 shorter events, 0.1 us)
Async XLA Ops:
  7.2 52.8 %all-gather.5.cloned.1.call-start = ((), (), s32[]{:S(2)}) async-start(), calls=%async_computation.4 | async-start | bytes 1114112 | tf_op jit(solution)/shard_map/all_gather | solution.py:156
  37.7 27.7 %all-to-all-start.1 = ((bf16[4,8,2,16,1024]{4,3,2,1,0:T(8,128)(2,1)}), bf16[4,8,2,16,1024]{4,3,2,1,0:T(8,128)(2,1)S(1)}, u32[]{:S(2)}, u32[]{:S(2)}) async-start(bf16[4,8,2,16,1024]{4,3,2,1,0:T(8,128)(2,1)} %broadcast_in_dim.7), calls=%async_computation.1 | async-start | bytes 4194304 | tf_op jit(solution)/shard_map/all_to_all | solution.py:25
  41.8 64.0 %all-gather.7.cloned.1.call-start = ((), (), s32[]{:S(2)}) async-start(), calls=%async_computation.5 | async-start | bytes 1114112 | tf_op jit(solution)/shard_map/all_gather | solution.py:176
  41.8 7.5 %collective-permute-start = (bf16[2,2,16,512]{3,2,1,0:T(8,128)(2,1)S(1)}, bf16[2,2,16,512]{3,2,1,0:T(8,128)(2,1)S(1)}, u32[]{:S(2)}, u32[]{:S(2)}) collective-permute-start(bf16[2,2,16,512]{3,2,1,0:T(8,128)(2,1)S(1)} %constant_dynamic-slice_fusion.1), channel_id=1, source_target_pairs={{0,0},{1,32},{2,64},{3,96},{4,1},{5,33},{6,65},{7,97},{8,128},{9,1... | collective-permute-start | bytes 196616 | tf_op jit(solution)/shard_map/ppermute | solution.py:175
  49.2 0.6 copy-start.10
  65.4 34.4 %copy-start = (bf16[4,8,2,16,1024]{4,3,2,1,0:T(8,128)(2,1)}, bf16[4,8,2,16,1024]{4,3,2,1,0:T(8,128)(2,1)S(1)}, u32[]{:S(2)}) copy-start(bf16[4,8,2,16,1024]{4,3,2,1,0:T(8,128)(2,1)S(1)} %all-to-all-done.1) | copy-start | bytes 6291460
  65.4 2.0 %copy-start.1 = (bf16[32,32,512]{2,1,0:T(8,128)(2,1)S(1)}, bf16[32,32,512]{2,1,0:T(8,128)(2,1)}, u32[]{:S(2)}) copy-start(bf16[32,32,512]{2,1,0:T(8,128)(2,1)} %all-gather.5.cloned.1.call-done) | copy-start | bytes 3145732
  70.2 1.0 copy-start.5
  71.2 0.8 copy-start.7
  72.0 1.0 copy-start.9
  73.0 32.8 %copy-start.2 = (bf16[32,32,512]{2,1,0:T(8,128)(2,1)S(1)}, bf16[32,32,512]{2,1,0:T(8,128)(2,1)}, u32[]{:S(2)}) copy-start(bf16[32,32,512]{2,1,0:T(8,128)(2,1)} %all-gather.5.cloned.1.call-done) | copy-start | bytes 3145732
  99.8 15.2 %all-to-all-start.3 = ((f32[16,16,256]{2,1,0:T(8,128)}), f32[16,16,256]{2,1,0:T(8,128)S(1)}, u32[]{:S(2)}, u32[]{:S(2)}) async-start(f32[16,16,256]{2,1,0:T(8,128)} %broadcast_in_dim.8), calls=%async_computation.3 | async-start | bytes 524288 | tf_op jit(solution)/shard_map/all_to_all | solution.py:25
  105.8 1.2 copy-start.3
  107.0 1.2 copy-start.4
  108.3 1.2 copy-start.6
  109.5 1.0 copy-start.8
Sparse Core Ops, SparseCore 0:
  10.7 49.2 all-gather.4
  62.1 40.7 all-gather.6

commit v2 on v1

v2 whole, which is shorter than its diff:
```python
import functools

import jax
import jax.numpy as jnp
from jax import lax
from jax.experimental import pallas as pl
from jax.experimental.pallas import tpu as pltpu
from jax.sharding import PartitionSpec as P

BW = 256
PANEL = 16
STEP = 128
X_COUNT, Z_COUNT = 4, 8
VMEM_LIMIT = 62 * 1024 * 1024

f32, bf16 = jnp.float32, jnp.bfloat16


def dot(left, right, left_dim, right_dim):
    return lax.dot_general(
        left, right, (((left_dim,), (right_dim,)), ((), ())), preferred_element_type=f32
    )


def spread(block, axis, count, groups=None):
    return lax.all_to_all(
        jnp.broadcast_to(block[None], (count,) + block.shape), axis, 0, 0, axis_index_groups=groups
    )


def start(*pairs, sem):
    copies = [pltpu.make_async_copy(*pair, sem.at[i]) for i, pair in enumerate(pairs)]
    for copy in copies:
        copy.start()
    return copies


def wait(copies):
    for copy in copies:
        copy.wait()


def diag_kernel(diag, c_diag, congruent, diag_in, c_out, sem):
    order = diag.shape[3]
    own, wide = c_diag.shape
    wait(start((diag, diag_in), sem=sem))
    a_diag = diag_in[:, 0].reshape(order, order)
    linv = diag_in[:, 1].reshape(order, order)
    inner = dot(linv, a_diag, 1, 0).astype(bf16)
    c_out[...] = dot(inner, linv, 1, 1).astype(bf16)
    copies = start((c_out, congruent), sem=sem)
    col = lax.axis_index("col")
    per = diag.shape[2] // own
    offset = pl.multiple_of(lax.rem(col, per) * own, own)
    linv_rows = diag_in[lax.div(col, per), 1, pl.ds(offset, own), :]
    c_rows = dot(linv_rows, inner, 1, 1).astype(bf16)
    target = lax.broadcasted_iota(jnp.int32, (order, wide), 1) + lax.axis_index("row") * wide
    pick = (lax.broadcasted_iota(jnp.int32, (order, wide), 0) == target).astype(bf16)
    c_diag[...] = dot(c_rows, pick, 1, 0).astype(bf16)
    wait(copies)


def band_kernel(
    diag, congruent, rows, first, panel, gram,
    linv_in, c_in, a_in, l_in, first_out, panel_out, gram_rows, sem,
):
    order, width = congruent.shape[0], rows.shape[3]
    band = panel.shape[0]
    blocks, pieces = band // diag.shape[2], band // rows.shape[2]
    copies = start(
        (rows.at[:, 1], l_in),
        (congruent.at[:, pl.ds(0, band)], c_in),
        (rows.at[pl.ds(0, pieces), 0], a_in),
        (diag.at[pl.ds(0, blocks), 1, :, pl.ds(0, band)], linv_in),
        sem=sem,
    )
    wait(copies[:2])
    half = 0.5 * dot(c_in[...], l_in[...].reshape(order, width), 0, 0)
    wait(copies[2:])
    solved = dot(linv_in[...].reshape(band, band), a_in[...].reshape(band, width), 1, 0)
    f = (solved - half).astype(bf16)
    first_out[...] = f
    p = (f.astype(f32) - half).astype(bf16)
    panel_out[...] = p
    copies = start((first_out, first), (panel_out, panel), sem=sem)
    copy_count, count = gram.shape[:2]
    per = 16 // count
    col = lax.axis_index("col")
    top = panel_out[pl.ds(pl.multiple_of(lax.div(col, per) * 16, 16), 16), :]
    gram_rows[...] = dot(top, p, 1, 1)
    own = gram_rows[pl.ds(pl.multiple_of(lax.rem(col, per) * count, count), count), :]
    for i in range(copy_count):
        gram[i] = own
    wait(copies)


def rest_kernel(
    diag, congruent, rows, panel, first, panel_cols,
    linv_in, c_in, rows_in, first_out, panel_all, sem,
):
    order, width = congruent.shape[0], rows.shape[3]
    band, own = panel.shape[0], panel_cols.shape[0]
    left = order - band
    blocks = band // diag.shape[2]
    copies = start(
        (rows, rows_in),
        (congruent.at[:, pl.ds(band, left)], c_in),
        (diag.at[pl.ds(blocks, diag.shape[0] - blocks), 1], linv_in),
        (panel, panel_all.at[pl.ds(0, band)]),
        sem=sem,
    )
    wait(copies)
    half = 0.5 * dot(c_in[...], rows_in[:, 1].reshape(order, width), 0, 0)
    solved = dot(linv_in[...].reshape(left, order), rows_in[:, 0].reshape(order, width), 1, 0)
    f = (solved - half).astype(bf16)
    first_out[...] = f
    copies = start((first_out, first), sem=sem)
    panel_all[pl.ds(band, left), :] = (f.astype(f32) - half).astype(bf16)
    offset = pl.multiple_of(lax.axis_index("col") * own, own)
    panel_cols[...] = panel_all[pl.ds(offset, own), :]
    wait(copies)


def split(x):
    high = x.astype(bf16)
    rest = x - high.astype(f32)
    middle = rest.astype(bf16)
    low = (rest - middle.astype(f32)).astype(bf16)
    return high, middle, low


def eliminate(scale, gram, g, w, beside):
    band = g.shape[0]
    g[...] = gram[...].reshape(band, band) * scale
    row_id = lax.broadcasted_iota(jnp.int32, (band, band), 0)
    col_id = lax.broadcasted_iota(jnp.int32, (band, band), 1)
    w[...] = jnp.where(row_id == col_id, 1.0, 0.0)
    tall = 2 * PANEL
    sub = lax.broadcasted_iota(jnp.int32, (tall, 128), 0)

    def load(row, size, lefts, rights):
        rows = pl.ds(row, size)
        return [g[rows, pl.ds(o, 128)] for o in lefts] + [w[rows, pl.ds(o, 128)] for o in rights]

    parts = load(0, tall, range(0, band, 128), range(0, 128, 128))
    for s in range(0, band, PANEL):
        left = s // 128 * 128
        right = (s // 128 + 1) * 128
        n_g = (band - left) // 128
        size = parts[0].shape[0]
        cols = [
            jnp.broadcast_to(parts[0][:, s - left + t : s - left + t + 1], (size, 128))
            for t in range(PANEL)
        ]
        pivots = jnp.zeros((PANEL, 128), f32)
        for j in range(PANEL):
            pivot = cols[j][j : j + 1, :]
            pivots = jnp.where(sub[:PANEL] == j, pivot, pivots)
            m = jnp.where(sub[:size] > j, cols[j] * (1.0 / pivot), 0.0)
            for t in range(j + 1, PANEL):
                cols[t] = cols[t] - m * cols[t][j : j + 1, :]
            parts = [part - m * part[j : j + 1, :] for part in parts]
        root = lax.rsqrt(pivots)
        near = [part[PANEL:] for part in parts]
        parts = [part[:PANEL] * root for part in parts]
        beside(s // PANEL)
        rows = pl.ds(s, PANEL)
        for i, o in enumerate(range(left, band, 128)):
            g[rows, pl.ds(o, 128)] = parts[i]
        for i, o in enumerate(range(0, right, 128)):
            w[rows, pl.ds(o, 128)] = parts[n_g + i]
        done = s + PANEL
        if done == band:
            break
        top = done // 128 * 128
        if top > left:
            near = near[1:] + [w[pl.ds(done, PANEL), pl.ds(right, 128)]]
        far = s + tall
        if far == band:
            parts = near
            continue
        u = jnp.concatenate(parts, axis=1)
        h, m, l = split(u)
        base = far // 128 * 128
        a, b = base - left, band - left
        lefts = jnp.concatenate([x[:, a:b] for x in (h, h, m, h, m, l)], axis=0)
        rights = jnp.concatenate([h, m, h, l, m, h], axis=0)
        update = dot(lefts, rights, 0, 0)[far - base :]
        entering = load(far, PANEL, range(top, band, 128), range(0, right, 128))
        entering = [
            x - update[:PANEL, o : o + 128]
            for x, o in zip(entering, range(top - left, update.shape[1], 128))
        ]
        if top > left:
            entering += [w[pl.ds(far, PANEL), pl.ds(right, 128)]]
        parts = [jnp.concatenate(pair, axis=0) for pair in zip(near, entering)]
        far += PANEL
        if far == band:
            continue
        rows = pl.ds(far, band - far)
        for o in range(top, band, 128):
            lanes = pl.ds(o, 128)
            g[rows, lanes] = g[rows, lanes] - update[PANEL:, o - left : o - left + 128]
        for o in range(0, right, 128):
            lanes = pl.ds(o, 128)
            w[rows, lanes] = w[rows, lanes] - update[PANEL:, b + o : b + o + 128]


def finish_kernel(
    scale, gram, panel, diag, congruent, rows, first_top, first_rest, cols, a_trail,
    r_cols, q_cols, c_trail,
    g, w, panel_in, linv_in, c_in, l_in, first_in, cols_in, a_in, first_cols, out, sem, out_sem,
):
    order = diag.shape[3]
    height = rows.shape[3]
    width = cols.shape[3]
    top = first_top.shape[0]
    copies = start(
        (cols, cols_in),
        (diag.at[:, 1], linv_in),
        (congruent, c_in),
        (first_top, first_in.at[pl.ds(0, top)]),
        (first_rest, first_in.at[pl.ds(top, order - top)]),
        (rows.at[:, 1], l_in),
        (a_trail, a_in),
        (panel, panel_in),
        sem=sem,
    )
    outs = []

    def first_of_columns():
        wait(copies[:3])
        a_cols = cols_in[:, 0].reshape(order, width)
        half = 0.5 * dot(c_in[...], cols_in[:, 1].reshape(order, width), 0, 0)
        solved = dot(linv_in[...].reshape(order, order), a_cols, 1, 0)
        first_cols[...] = (solved - half).astype(bf16)

    def trail(i):
        if i == 0:
            wait(copies[3:7])
        part = pl.ds(i * STEP, STEP)
        l_rows = l_in[:, :, part].reshape(order, STEP)
        update = dot(first_in[:, part], cols_in[:, 1].reshape(order, width), 0, 0)
        update += dot(l_rows, first_cols[...], 0, 0)
        out[part] = (a_in[part].astype(f32) - update).astype(bf16)
        outs.extend(start((out.at[part], c_trail.at[part]), sem=out_sem.at[pl.ds(i, 1)]))

    def beside(i):
        if i == 1:
            first_of_columns()
        if 2 <= i < 2 + height // STEP:
            trail(i - 2)

    eliminate(scale, gram, g, w, beside)
    band = g.shape[0]
    count = q_cols.shape[0]
    offset = pl.multiple_of(lax.axis_index("col") * count, count)
    inverse = jnp.concatenate(list(split(w[pl.ds(offset, count), :])), axis=0)
    wait(copies[7:])
    q = dot(inverse, panel_in[...], 1, 0)
    q_cols[...] = q[:count] + q[count : 2 * count] + q[2 * count :]
    own = r_cols.shape[1]
    offset = pl.multiple_of(lax.axis_index("row") * own, own)
    column = lax.broadcasted_iota(jnp.int32, (own, band), 1)
    row = lax.broadcasted_iota(jnp.int32, (own, band), 0) + offset
    upper = jnp.where(column >= row, g[pl.ds(offset, own), :], 0.0)
    target = lax.broadcasted_iota(jnp.int32, (count, band), 0) + lax.axis_index("col") * count
    pick = (lax.broadcasted_iota(jnp.int32, (count, band), 1) == target).astype(bf16)
    high, middle, low = (dot(pick, x, 1, 1) for x in split(upper))
    r_cols[...] = high + (middle + low)
    wait(outs)


def call(kernel, cost, ins, outs, *operands, scratch=()):
    return pl.pallas_call(
        kernel,
        out_shape=[jax.ShapeDtypeStruct(shape, dtype) for _, shape, dtype in outs],
        in_specs=[pl.BlockSpec(memory_space=space) for space in ins],
        out_specs=[pl.BlockSpec(memory_space=space) for space, _, _ in outs],
        scratch_shapes=list(scratch),
        cost_estimate=pl.CostEstimate(flops=cost, bytes_accessed=cost // 500, transcendentals=0),
        compiler_params=pltpu.CompilerParams(vmem_limit_bytes=VMEM_LIMIT),
    )(*operands)


def body(a_trail, a_panel, l_panel, a_diag, linv_diag):
    row_count = lax.axis_size("row")
    col_count = lax.axis_size("col")
    col_index = lax.axis_index("col")
    x_index, z_index = col_index // Z_COUNT, col_index % Z_COUNT
    z_groups = [[x * Z_COUNT + z for z in range(Z_COUNT)] for x in range(X_COUNT)]
    x_groups = [[x * Z_COUNT + z for x in range(X_COUNT)] for z in range(Z_COUNT)]
    height, own = a_panel.shape
    order = a_diag.shape[1]
    width = a_trail.shape[1]

    diag = lax.all_gather(jnp.stack((a_diag, linv_diag)), "row", axis=0)

    pair = jnp.stack((a_panel.T, l_panel.T))
    by_z = spread(pair, "col", Z_COUNT, z_groups)
    rows = spread(by_z, "col", X_COUNT, x_groups).reshape(col_count, 2, own, height)

    halves = height // width
    piece = Z_COUNT // (Z_COUNT // halves)
    per = Z_COUNT // halves
    half_index, quarter = z_index // per, z_index % per
    share = lax.dynamic_slice(
        by_z, (quarter * piece, 0, 0, half_index * width), (piece, 2, own, width)
    )
    moves = []
    for r in range(row_count):
        for c in range(col_count):
            x, z = c // Z_COUNT, c % Z_COUNT
            target = (x * per + z % per) * col_count + r * halves + z // per
            moves.append((r * col_count + c, target))
    share = lax.ppermute(share, ("row", "col"), moves)
    cols = lax.all_gather(share, "row", axis=0).reshape(col_count, 2, own, width)

    HBM, VMEM = pltpu.HBM, pltpu.VMEM
    band_rows, band_cols = BW // row_count, BW // col_count
    diag_rows = a_diag.shape[0]
    sems = pltpu.SemaphoreType.DMA
    c_diag, congruent = call(
        diag_kernel,
        2 * 2 * order**3,
        [HBM],
        [(VMEM, (own, diag_rows), bf16), (HBM, (order, order), bf16)],
        diag,
        scratch=[VMEM(diag.shape, bf16), VMEM((order, order), bf16), sems((1,))],
    )
    first_top, panel_top, gram = call(
        band_kernel,
        2 * 2 * order * height * BW,
        [HBM] * 3,
        [
            (HBM, (BW, height), bf16),
            (HBM, (BW, height), bf16),
            (VMEM, (row_count, band_cols, BW), f32),
        ],
        diag,
        congruent,
        rows,
        scratch=[
            VMEM((BW // diag_rows, diag_rows, BW), bf16),
            VMEM((order, BW), bf16),
            VMEM((BW // own, own, height), bf16),
            VMEM((col_count, own, height), bf16),
            VMEM((BW, height), bf16),
            VMEM((BW, height), bf16),
            VMEM((16, BW), f32),
            sems((4,)),
        ],
    )
    left = order - BW
    first_rest, panel_cols = call(
        rest_kernel,
        2 * 2 * order * height * left,
        [HBM] * 4,
        [(HBM, (left, height), bf16), (VMEM, (own, height), bf16)],
        diag,
        congruent,
        rows,
        panel_top,
        scratch=[
            VMEM((left // diag_rows, diag_rows, order), bf16),
            VMEM((order, left), bf16),
            VMEM(rows.shape, bf16),
            VMEM((left, height), bf16),
            VMEM((order, height), bf16),
            sems((4,)),
        ],
    )
    gram = lax.all_to_all(gram, "row", 0, 0).sum(axis=0)
    gram = spread(gram, "col", col_count)
    r_cols, q_cols, c_trail = call(
        functools.partial(finish_kernel, 1.0 / (height * row_count)),
        2 * 2 * (height + width) * width * order,
        [VMEM] + [HBM] * 8,
        [
            (VMEM, (band_cols, band_rows), f32),
            (VMEM, (band_cols, height), f32),
            (HBM, a_trail.shape, bf16),
        ],
        gram,
        panel_top,
        diag,
        congruent,
        rows,
        first_top,
        first_rest,
        cols,
        a_trail,
        scratch=[
            VMEM((BW, BW), f32),
            VMEM((BW, BW), f32),
            VMEM((BW, height), bf16),
            VMEM((row_count, diag_rows, order), bf16),
            VMEM((order, order), bf16),
            VMEM((col_count, own, height), bf16),
            VMEM((order, height), bf16),
            VMEM(cols.shape, bf16),
            VMEM(a_trail.shape, bf16),
            VMEM((order, width), bf16),
            VMEM(a_trail.shape, bf16),
            sems((8,)),
            sems((height // STEP,)),
        ],
    )
    return (c_trail, panel_cols.T, c_diag.T, r_cols.T, q_cols.T)


def solution(mesh):
    both = P("row", "col")
    return jax.shard_map(
        body,
        mesh=mesh,
        in_specs=(both, both, both, P("row", None), P("row", None)),
        out_specs=(both, both, both, both, both),
        check_vma=False,
    )
```

time: 132 us -> 127 us (0.962)
  local copies, waits for them, and re-layouts: 15.7 us -> 3.73 us
  Pallas kernels: 15.5 us -> 21.9 us
  waiting for transfers between devices: 18.7 us -> 22.5 us
  blocking collectives: 52.6 us -> 49.3 us
    unnamed x24 -> x4, local copies, waits for them, and re-layouts: 11.4 us -> 1.35 us
    pallas_call x3 -> x4, Pallas kernels: 15.5 us -> 21.9 us  [call(): pl.pallas_call(kernel, out_shape=[jax.ShapeDtypeStruct(shape, dtype) for...]
    all_to_all x1, blocking collectives: 26.1 us -> 22.7 us  [body(): gram = lax.all_to_all(gram, 'row', 0, 0).sum(axis=0)]
    all_to_all x2, waiting for transfers between devices: 5.44 us -> 8.19 us  [spread(): lax.all_to_all(jnp.broadcast_to(block[None], (count,) + block.shape), axi...]
  transfers between devices with their start and end apart: 5 -> 5, of which waited for: 3 -> 5; matrix products, arithmetic and copies ran while one was open for 4% -> 3% of each run, Pallas kernels for 6% -> 9%
where the time goes in v2:
time: 127 us; the launch traced here: 126 us
  blocking collectives  49.3 us (39%)
  waiting for transfers between devices  22.5 us (18%)
  Pallas kernels  21.9 us (17%)
  between operations  14.2 us (11%)
  starting transfers between devices  12.5 us (10%)
  local copies, waits for them, and re-layouts  3.73 us (3%)
  other arithmetic  2.21 us (2%)
    all_to_all x1, blocking collectives, spread(): lax.all_to_all(jnp.broadcast_to(block[None], (count,) + block.shape), axi...  26.6 us
    all_to_all x1, blocking collectives, body(): gram = lax.all_to_all(gram, 'row', 0, 0).sum(axis=0)  22.7 us
    pallas_call x4, Pallas kernels, call(): pl.pallas_call(kernel, out_shape=[jax.ShapeDtypeStruct(shape, dtype) for...  21.9 us
    all_gather x1, waiting for transfers between devices, body(): diag = lax.all_gather(jnp.stack((a_diag, linv_diag)), 'row', axis=0)  10.1 us
    all_to_all x2, starting transfers between devices, spread(): lax.all_to_all(jnp.broadcast_to(block[None], (count,) + block.shape), axi...  8.33 us
    all_to_all x2, waiting for transfers between devices, spread(): lax.all_to_all(jnp.broadcast_to(block[None], (count,) + block.shape), axi...  8.19 us
    ppermute x1, starting transfers between devices, body(): share = lax.ppermute(share, ('row', 'col'), moves)  4.13 us
    ppermute x1, waiting for transfers between devices, body(): share = lax.ppermute(share, ('row', 'col'), moves)  3.04 us
  transfers between devices with their start and end apart: 5, of which 5 were waited for; matrix products, arithmetic and copies ran while one was open for 3% of the time, Pallas kernels for 9%

profile of v2, /device:TPU:1, one launch (start us, length us, event | category | flops | bytes accessed | tf_op | source)
XLA Modules:
  0.0 126.3 jit_solution(2245598358326284174)
XLA Ops:
  7.2 0.0 all-gather.5.cloned.1.call-start
  7.2 1.4 %pad_maximum_fusion = bf16[2,32,512]{2,1,0:T(8,128)(2,1)} fusion(bf16[1,32,512]{2,1,0:T(8,128)(2,1)} %bitcast.18, bf16[1,32,512]{2,1,0:T(8,128)(2,1)} %bitcast.19), kind=kLoop, calls=%fused_computation | loop fusion | flops 32768 | bytes 131072 | tf_op jit(solution)/shard_map/stack | solution.py:297
  8.6 0.0 all-gather.5.cloned.1.call-update
  8.6 0.8 pad_maximum_fusion.1
  9.5 26.6 %all_to_all.20 = bf16[8,2,16,1024]{3,2,1,0:T(8,128)(2,1)S(1)} all-to-all(bf16[8,2,16,1024]{3,2,1,0:T(8,128)(2,1)S(1)} %broadcast_in_dim.6), channel_id=1, replica_groups={{0,1,2,3,4,5,6,7},{8,9,10,11,12,13,14,15},{16,17,18,19,20,21,22,23},{24..., dimensions={0} | all-to-all | bytes 1048576 | tf_op jit(solution)/shard_map/all_to_all | solution.py:26
  36.1 1.6 %broadcast_in_dim.7 = bf16[4,8,2,16,1024]{4,3,2,1,0:T(8,128)(2,1)} broadcast(bf16[8,2,16,1024]{3,2,1,0:T(8,128)(2,1)S(1)} %all_to_all.20), dimensions={1,2,3,4} | broadcast | bytes 2621440 | tf_op jit(solution)/shard_map/broadcast_in_dim | solution.py:27
  37.7 4.5 %all-to-all-start.1 = ((bf16[4,8,2,16,1024]{4,3,2,1,0:T(8,128)(2,1)}), bf16[4,8,2,16,1024]{4,3,2,1,0:T(8,128)(2,1)}, u32[]{:S(2)}, u32[]{:S(2)}) async-start(bf16[4,8,2,16,1024]{4,3,2,1,0:T(8,128)(2,1)} %broadcast_in_dim.7), calls=%async_computation.1 | async-start | bytes 4194304 | tf_op jit(solution)/shard_map/all_to_all | solution.py:26
  42.1 0.0 all-gather.7.cloned.1.call-start
  42.2 4.1 %collective-permute-start = (bf16[2,2,16,512]{3,2,1,0:T(8,128)(2,1)S(1)}, bf16[2,2,16,512]{3,2,1,0:T(8,128)(2,1)S(1)}, u32[]{:S(2)}, u32[]{:S(2)}) collective-permute-start(bf16[2,2,16,512]{3,2,1,0:T(8,128)(2,1)S(1)} %constant_dynamic-slice_fusion), channel_id=1, source_target_pairs={{0,0},{1,32},{2,64},{3,96},{4,1},{5,33},{6,65},{7,97},{8,128},{9,1... | collective-permute-start | bytes 196616 | tf_op jit(solution)/shard_map/ppermute | solution.py:316
  46.4 3.0 %collective-permute-done = bf16[2,2,16,512]{3,2,1,0:T(8,128)(2,1)S(1)} collective-permute-done((bf16[2,2,16,512]{3,2,1,0:T(8,128)(2,1)S(1)}, bf16[2,2,16,512]{3,2,1,0:T(8,128)(2,1)S(1)}, u32[]{:S(2)}, u32[]{:S(2)}) %collective-permute-start) | collective-permute-done | bytes 65568 | tf_op jit(solution)/shard_map/ppermute | solution.py:316
  49.4 0.0 copy-start.1
  49.4 0.6 copy-done.1
  50.0 0.0 all-gather.7.cloned.1.call-update
  50.1 10.1 %all-gather.5.cloned.1.call-done = bf16[32,32,512]{2,1,0:T(8,128)(2,1)} async-done(((bf16[2,32,512]{2,1,0:T(8,128)(2,1)}), bf16[32,32,512]{2,1,0:T(8,128)(2,1)}) %all-gather.5.cloned.1.call-update) | async-done | bytes 1048592 | tf_op jit(solution)/shard_map/all_gather | solution.py:297
  60.2 3.3 %shard_map.92 = (bf16[16,32]{1,0:T(8,128)(2,1)}, bf16[512,512]{1,0:T(8,128)(2,1)}) custom-call(bf16[16,2,32,512]{3,2,1,0:T(8,128)(2,1)} %bitcast.14), custom_call_target="tpu_custom_call" | custom-call | flops 536870912 | bytes 1073741 | tf_op jit(solution)/shard_map/pallas_call | solution.py:275
  63.5 2.5 %all-to-all-done.1 = bf16[4,8,2,16,1024]{4,3,2,1,0:T(8,128)(2,1)} async-done(((bf16[4,8,2,16,1024]{4,3,2,1,0:T(8,128)(2,1)}), bf16[4,8,2,16,1024]{4,3,2,1,0:T(8,128)(2,1)}, u32[]{:S(2)}, u32[]{:S(2)}) %all-to-all-start.1) | async-done | bytes 2097184 | tf_op jit(solution)/shard_map/all_to_all | solution.py:26
  66.0 3.8 %shard_map.93 = (bf16[256,1024]{1,0:T(8,128)(2,1)}, bf16[256,1024]{1,0:T(8,128)(2,1)}, f32[16,8,256]{2,1,0:T(8,128)}) custom-call(bf16[16,2,32,512]{3,2,1,0:T(8,128)(2,1)} %bitcast.15, bf16[512,512]{1,0:T(8,128)(2,1)} %get-tuple-element.15.congruent, bf16[32,2,16,1024]{3,2,1,0:T(8,128)(2,1)} %bitcast.7.rows), custom_call_target="tpu_custom_call" | custom-call | flops 536870912 | bytes 1073741 | tf_op jit(solution)/shard_map/pallas_call | solution.py:275
  69.9 22.7 %all_to_all.21 = f32[16,8,256]{2,1,0:T(8,128)S(1)} all-to-all(f32[16,8,256]{2,1,0:T(8,128)} %get-tuple-element.16), channel_id=1, replica_groups=mesh['row'=16,'col'=32] {'row'}, dimensions={0} | all-to-all | bytes 262144 | tf_op jit(solution)/shard_map/all_to_all | solution.py:373
  92.6 0.7 broadcast_in_dim.8
  93.3 3.9 %all-to-all-start.3 = ((f32[32,8,256]{2,1,0:T(8,128)}), f32[32,8,256]{2,1,0:T(8,128)S(1)}, u32[]{:S(2)}, u32[]{:S(2)}) async-start(f32[32,8,256]{2,1,0:T(8,128)} %broadcast_in_dim.8), calls=%async_computation.3 | async-start | bytes 524288 | tf_op jit(solution)/shard_map/all_to_all | solution.py:26
  97.2 4.1 %shard_map.94 = (bf16[256,1024]{1,0:T(8,128)(2,1)}, bf16[16,1024]{1,0:T(8,128)(2,1)}) custom-call(bf16[16,2,32,512]{3,2,1,0:T(8,128)(2,1)} %bitcast.16, bf16[512,512]{1,0:T(8,128)(2,1)} %get-tuple-element.15.congruent, bf16[32,2,16,1024]{3,2,1,0:T(8,128)(2,1)} %bitcast.7.rows, bf16[256,1024]{1,0:T(8,128)(2,1)} %get-tuple-element.17.panel), custom_call_target="tpu_custom_call" | custom-call | flops 536870912 | bytes 1073741 | tf_op jit(solution)/shard_map/pallas_call | solution.py:275
  101.3 1.1 all-gather.7.cloned.1.call-done.cols
  102.4 5.7 %all-to-all-done.3.gram = f32[32,8,256]{2,1,0:T(8,128)S(1)} async-done(((f32[32,8,256]{2,1,0:T(8,128)}), f32[32,8,256]{2,1,0:T(8,128)S(1)}, u32[]{:S(2)}, u32[]{:S(2)}) %all-to-all-start.3) | async-done | bytes 262176 | tf_op jit(solution)/shard_map/all_to_all | solution.py:26
  108.1 0.0 copy-start
  108.1 0.7 copy-done
  108.8 10.6 %shard_map.95 = (f32[8,16]{1,0:T(8,128)}, f32[8,1024]{1,0:T(8,128)}, bf16[1024,512]{1,0:T(8,128)(2,1)}) custom-call(f32[32,8,256]{2,1,0:T(8,128)} %copy-done, bf16[256,1024]{1,0:T(8,128)(2,1)} %get-tuple-element.17.panel, bf16[16,2,32,512]{3,2,1,0:T(8,128)(2,1)} %bitcast.17, bf16[512,512]{1,0:T(8,128)(2,1)} %get-tuple-element.15.congruent, ...), custom_call_target="tpu_custom_call" | custom-call | flops 1610612736 | bytes 3221225 | tf_op jit(solution)/shard_map/pallas_call | solution.py:275
  (3 shorter events, 0.1 us)
Async XLA Ops:
  7.2 53.0 %all-gather.5.cloned.1.call-start = ((), (), s32[]{:S(2)}) async-start(), calls=%async_computation.4 | async-start | bytes 1114112 | tf_op jit(solution)/shard_map/all_gather | solution.py:297
  37.7 28.4 %all-to-all-start.1 = ((bf16[4,8,2,16,1024]{4,3,2,1,0:T(8,128)(2,1)}), bf16[4,8,2,16,1024]{4,3,2,1,0:T(8,128)(2,1)}, u32[]{:S(2)}, u32[]{:S(2)}) async-start(bf16[4,8,2,16,1024]{4,3,2,1,0:T(8,128)(2,1)} %broadcast_in_dim.7), calls=%async_computation.1 | async-start | bytes 4194304 | tf_op jit(solution)/shard_map/all_to_all | solution.py:26
  42.1 60.3 %all-gather.7.cloned.1.call-start = ((), (), s32[]{:S(2)}) async-start(), calls=%async_computation.5 | async-start | bytes 1114112 | tf_op jit(solution)/shard_map/all_gather | solution.py:317
  42.2 7.2 %collective-permute-start = (bf16[2,2,16,512]{3,2,1,0:T(8,128)(2,1)S(1)}, bf16[2,2,16,512]{3,2,1,0:T(8,128)(2,1)S(1)}, u32[]{:S(2)}, u32[]{:S(2)}) collective-permute-start(bf16[2,2,16,512]{3,2,1,0:T(8,128)(2,1)S(1)} %constant_dynamic-slice_fusion), channel_id=1, source_target_pairs={{0,0},{1,32},{2,64},{3,96},{4,1},{5,33},{6,65},{7,97},{8,128},{9,1... | collective-permute-start | bytes 196616 | tf_op jit(solution)/shard_map/ppermute | solution.py:316
  49.4 0.6 copy-start.1
  93.3 14.8 %all-to-all-start.3 = ((f32[32,8,256]{2,1,0:T(8,128)}), f32[32,8,256]{2,1,0:T(8,128)S(1)}, u32[]{:S(2)}, u32[]{:S(2)}) async-start(f32[32,8,256]{2,1,0:T(8,128)} %broadcast_in_dim.8), calls=%async_computation.3 | async-start | bytes 524288 | tf_op jit(solution)/shard_map/all_to_all | solution.py:26
  108.1 0.7 copy-start
Sparse Core Ops, SparseCore 0:
  10.7 49.4 all-gather.4
  62.3 40.1 all-gather.6

commit v3 on v2

--- a/solution.py
+++ b/solution.py
@@ -40,42 +40,51 @@
         copy.wait()
 
 
-def diag_kernel(diag, c_diag, congruent, diag_in, c_out, sem):
+def prepare_kernel(a_diag, linv_diag, a_panel, l_panel, diag, pairs, diag_in, pair_in, sem, out_sem):
+    copies = start(
+        (a_diag, diag_in.at[0]),
+        (linv_diag, diag_in.at[1]),
+        (a_panel, pair_in.at[0]),
+        (l_panel, pair_in.at[1]),
+        sem=sem,
+    )
+    wait(copies)
+    outs = [(diag_in, diag)] + [(pair_in, pairs.at[i]) for i in range(pairs.shape[0])]
+    wait(start(*outs, sem=out_sem))
+
+
+def diag_kernel(diag, c_diag, turned, diag_in, turned_out, sem):
     order = diag.shape[3]
     own, wide = c_diag.shape
     wait(start((diag, diag_in), sem=sem))
     a_diag = diag_in[:, 0].reshape(order, order)
     linv = diag_in[:, 1].reshape(order, order)
     inner = dot(linv, a_diag, 1, 0).astype(bf16)
-    c_out[...] = dot(inner, linv, 1, 1).astype(bf16)
-    copies = start((c_out, congruent), sem=sem)
-    col = lax.axis_index("col")
-    per = diag.shape[2] // own
-    offset = pl.multiple_of(lax.rem(col, per) * own, own)
-    linv_rows = diag_in[lax.div(col, per), 1, pl.ds(offset, own), :]
-    c_rows = dot(linv_rows, inner, 1, 1).astype(bf16)
+    turned_out[...] = dot(linv, inner, 1, 1).astype(bf16)
+    copies = start((turned_out, turned), sem=sem)
+    offset = pl.multiple_of(lax.axis_index("col") * own, own)
     target = lax.broadcasted_iota(jnp.int32, (order, wide), 1) + lax.axis_index("row") * wide
     pick = (lax.broadcasted_iota(jnp.int32, (order, wide), 0) == target).astype(bf16)
-    c_diag[...] = dot(c_rows, pick, 1, 0).astype(bf16)
+    c_diag[...] = dot(turned_out[pl.ds(offset, own), :], pick, 1, 0).astype(bf16)
     wait(copies)
 
 
 def band_kernel(
-    diag, congruent, rows, first, panel, gram,
+    diag, turned, rows, first, panel, gram,
     linv_in, c_in, a_in, l_in, first_out, panel_out, gram_rows, sem,
 ):
-    order, width = congruent.shape[0], rows.shape[3]
+    order, width = turned.shape[0], rows.shape[3]
     band = panel.shape[0]
     blocks, pieces = band // diag.shape[2], band // rows.shape[2]
     copies = start(
         (rows.at[:, 1], l_in),
-        (congruent.at[:, pl.ds(0, band)], c_in),
+        (turned.at[pl.ds(0, band)], c_in),
         (rows.at[pl.ds(0, pieces), 0], a_in),
         (diag.at[pl.ds(0, blocks), 1, :, pl.ds(0, band)], linv_in),
         sem=sem,
     )
     wait(copies[:2])
-    half = 0.5 * dot(c_in[...], l_in[...].reshape(order, width), 0, 0)
+    half = 0.5 * dot(c_in[...], l_in[...].reshape(order, width), 1, 0)
     wait(copies[2:])
     solved = dot(linv_in[...].reshape(band, band), a_in[...].reshape(band, width), 1, 0)
     f = (solved - half).astype(bf16)
@@ -95,30 +104,38 @@
 
 
 def rest_kernel(
-    diag, congruent, rows, panel, first, panel_cols,
-    linv_in, c_in, rows_in, first_out, panel_all, sem,
+    diag, turned, rows, first, panel, first_rows, panel_cols,
+    linv_in, c_in, rows_in, first_all, panel_all, first_out, sem,
 ):
-    order, width = congruent.shape[0], rows.shape[3]
+    order, width = turned.shape[0], rows.shape[3]
     band, own = panel.shape[0], panel_cols.shape[0]
     left = order - band
     blocks = band // diag.shape[2]
     copies = start(
         (rows, rows_in),
-        (congruent.at[:, pl.ds(band, left)], c_in),
+        (turned.at[pl.ds(band, left)], c_in),
         (diag.at[pl.ds(blocks, diag.shape[0] - blocks), 1], linv_in),
+        (first, first_all.at[pl.ds(0, band)]),
         (panel, panel_all.at[pl.ds(0, band)]),
         sem=sem,
     )
     wait(copies)
-    half = 0.5 * dot(c_in[...], rows_in[:, 1].reshape(order, width), 0, 0)
+    half = 0.5 * dot(c_in[...], rows_in[:, 1].reshape(order, width), 1, 0)
     solved = dot(linv_in[...].reshape(left, order), rows_in[:, 0].reshape(order, width), 1, 0)
     f = (solved - half).astype(bf16)
-    first_out[...] = f
-    copies = start((first_out, first), sem=sem)
+    first_all[pl.ds(band, left), :] = f
     panel_all[pl.ds(band, left), :] = (f.astype(f32) - half).astype(bf16)
+    first_out[...] = first_all[...].T
+    copies = start((first_out, first_rows), sem=sem)
     offset = pl.multiple_of(lax.axis_index("col") * own, own)
     panel_cols[...] = panel_all[pl.ds(offset, own), :]
     wait(copies)
+
+
+def turn_kernel(rows, l_rows, l_in, l_out, sem):
+    wait(start((rows.at[:, 1], l_in), sem=sem))
+    l_out[...] = l_in[...].reshape(l_rows.shape[1], l_rows.shape[0]).T
+    wait(start((l_out, l_rows), sem=sem))
 
 
 def split(x):
@@ -207,21 +224,20 @@
 
 
 def finish_kernel(
-    scale, gram, panel, diag, congruent, rows, first_top, first_rest, cols, a_trail,
+    scale, gram, panel, diag, turned, first, l_rows, cols, a_trail,
     r_cols, q_cols, c_trail,
-    g, w, panel_in, linv_in, c_in, l_in, first_in, cols_in, a_in, first_cols, out, sem, out_sem,
+    g, w, gram_in, panel_in, linv_in, c_in, l_in, first_in, cols_in, a_in, first_cols, out,
+    sem, out_sem,
 ):
     order = diag.shape[3]
-    height = rows.shape[3]
-    width = cols.shape[3]
-    top = first_top.shape[0]
+    height, width = a_trail.shape
     copies = start(
+        (gram, gram_in),
         (cols, cols_in),
         (diag.at[:, 1], linv_in),
-        (congruent, c_in),
-        (first_top, first_in.at[pl.ds(0, top)]),
-        (first_rest, first_in.at[pl.ds(top, order - top)]),
-        (rows.at[:, 1], l_in),
+        (turned, c_in),
+        (first, first_in),
+        (l_rows, l_in),
         (a_trail, a_in),
         (panel, panel_in),
         sem=sem,
@@ -229,19 +245,18 @@
     outs = []
 
     def first_of_columns():
-        wait(copies[:3])
+        wait(copies[1:4])
         a_cols = cols_in[:, 0].reshape(order, width)
-        half = 0.5 * dot(c_in[...], cols_in[:, 1].reshape(order, width), 0, 0)
+        half = 0.5 * dot(c_in[...], cols_in[:, 1].reshape(order, width), 1, 0)
         solved = dot(linv_in[...].reshape(order, order), a_cols, 1, 0)
         first_cols[...] = (solved - half).astype(bf16)
 
     def trail(i):
         if i == 0:
-            wait(copies[3:7])
+            wait(copies[4:7])
         part = pl.ds(i * STEP, STEP)
-        l_rows = l_in[:, :, part].reshape(order, STEP)
-        update = dot(first_in[:, part], cols_in[:, 1].reshape(order, width), 0, 0)
-        update += dot(l_rows, first_cols[...], 0, 0)
+        update = dot(first_in[part], cols_in[:, 1].reshape(order, width), 1, 0)
+        update += dot(l_in[part], first_cols[...], 1, 0)
         out[part] = (a_in[part].astype(f32) - update).astype(bf16)
         outs.extend(start((out.at[part], c_trail.at[part]), sem=out_sem.at[pl.ds(i, 1)]))
 
@@ -251,7 +266,8 @@
         if 2 <= i < 2 + height // STEP:
             trail(i - 2)
 
-    eliminate(scale, gram, g, w, beside)
+    wait(copies[:1])
+    eliminate(scale, gram_in, g, w, beside)
     band = g.shape[0]
     count = q_cols.shape[0]
     offset = pl.multiple_of(lax.axis_index("col") * count, count)
@@ -294,10 +310,27 @@
     order = a_diag.shape[1]
     width = a_trail.shape[1]
 
-    diag = lax.all_gather(jnp.stack((a_diag, linv_diag)), "row", axis=0)
-
-    pair = jnp.stack((a_panel.T, l_panel.T))
-    by_z = spread(pair, "col", Z_COUNT, z_groups)
+    HBM, VMEM = pltpu.HBM, pltpu.VMEM
+    sems = pltpu.SemaphoreType.DMA
+    diag_rows = a_diag.shape[0]
+    diag, pairs = call(
+        prepare_kernel,
+        1 << 20,
+        [HBM] * 4,
+        [(HBM, (2, diag_rows, order), bf16), (HBM, (Z_COUNT, 2, own, height), bf16)],
+        a_diag,
+        linv_diag,
+        a_panel.T,
+        l_panel.T,
+        scratch=[
+            VMEM((2, diag_rows, order), bf16),
+            VMEM((2, own, height), bf16),
+            sems((4,)),
+            sems((1 + Z_COUNT,)),
+        ],
+    )
+    diag = lax.all_gather(diag, "row", axis=0)
+    by_z = lax.all_to_all(pairs, "col", 0, 0, axis_index_groups=z_groups)
     rows = spread(by_z, "col", X_COUNT, x_groups).reshape(col_count, 2, own, height)
 
     halves = height // width
@@ -316,11 +349,8 @@
     share = lax.ppermute(share, ("row", "col"), moves)
     cols = lax.all_gather(share, "row", axis=0).reshape(col_count, 2, own, width)
 
-    HBM, VMEM = pltpu.HBM, pltpu.VMEM
     band_rows, band_cols = BW // row_count, BW // col_count
-    diag_rows = a_diag.shape[0]
-    sems = pltpu.SemaphoreType.DMA
-    c_diag, congruent = call(
+    c_diag, turned = call(
         diag_kernel,
         2 * 2 * order**3,
         [HBM],
@@ -338,11 +368,11 @@
             (VMEM, (row_count, band_cols, BW), f32),
         ],
         diag,
-        congruent,
+        turned,
         rows,
         scratch=[
             VMEM((BW // diag_rows, diag_rows, BW), bf16),
-            VMEM((order, BW), bf16),
+            VMEM((BW, order), bf16),
             VMEM((BW // own, own, height), bf16),
             VMEM((col_count, own, height), bf16),
             VMEM((BW, height), bf16),
@@ -352,22 +382,36 @@
         ],
     )
     left = order - BW
-    first_rest, panel_cols = call(
+    first, panel_cols = call(
         rest_kernel,
         2 * 2 * order * height * left,
-        [HBM] * 4,
-        [(HBM, (left, height), bf16), (VMEM, (own, height), bf16)],
+        [HBM] * 5,
+        [(HBM, (height, order), bf16), (VMEM, (own, height), bf16)],
         diag,
-        congruent,
+        turned,
         rows,
+        first_top,
         panel_top,
         scratch=[
             VMEM((left // diag_rows, diag_rows, order), bf16),
-            VMEM((order, left), bf16),
+            VMEM((left, order), bf16),
             VMEM(rows.shape, bf16),
-            VMEM((left, height), bf16),
             VMEM((order, height), bf16),
-            sems((4,)),
+            VMEM((order, height), bf16),
+            VMEM((height, order), bf16),
+            sems((5,)),
+        ],
+    )
+    (l_rows,) = call(
+        turn_kernel,
+        order * height * 1000,
+        [HBM],
+        [(HBM, (height, order), bf16)],
+        rows,
+        scratch=[
+            VMEM((col_count, own, height), bf16),
+            VMEM((height, order), bf16),
+            sems((1,)),
         ],
     )
     gram = lax.all_to_all(gram, "row", 0, 0).sum(axis=0)
@@ -375,7 +419,7 @@
     r_cols, q_cols, c_trail = call(
         functools.partial(finish_kernel, 1.0 / (height * row_count)),
         2 * 2 * (height + width) * width * order,
-        [VMEM] + [HBM] * 8,
+        [HBM] * 8,
         [
             (VMEM, (band_cols, band_rows), f32),
             (VMEM, (band_cols, height), f32),
@@ -384,20 +428,20 @@
         gram,
         panel_top,
         diag,
-        congruent,
-        rows,
-        first_top,
-        first_rest,
+        turned,
+        first,
+        l_rows,
         cols,
         a_trail,
         scratch=[
             VMEM((BW, BW), f32),
             VMEM((BW, BW), f32),
+            VMEM(gram.shape, f32),
             VMEM((BW, height), bf16),
             VMEM((row_count, diag_rows, order), bf16),
             VMEM((order, order), bf16),
-            VMEM((col_count, own, height), bf16),
-            VMEM((order, height), bf16),
+            VMEM((height, order), bf16),
+            VMEM((height, order), bf16),
             VMEM(cols.shape, bf16),
             VMEM(a_trail.shape, bf16),
             VMEM((order, width), bf16),

time: 127 us -> 125 us (0.984)
  Pallas kernels: 21.9 us -> 24.9 us
  waiting for transfers between devices: 22.5 us -> 19.5 us
  other arithmetic: 2.21 us -> 0.02 us
    pallas_call x4 -> x6, Pallas kernels: 21.9 us -> 24.9 us  [call(): pl.pallas_call(kernel, out_shape=[jax.ShapeDtypeStruct(shape, dtype) for...]
    another operation x2 -> x0, other arithmetic: 2.2 us -> none  [the longest x1 1.41 us: body(): diag = lax.all_gather(jnp.stack((a_diag, linv_diag)), 'row', axis=0)]
    all_to_all x2, waiting for transfers between devices: 8.19 us -> 6.31 us  [spread(): lax.all_to_all(jnp.broadcast_to(block[None], (count,) + block.shape), axi...]
  transfers between devices with their start and end apart: 5 -> 5, of which waited for: 5 -> 4; matrix products, arithmetic and copies ran while one was open for 3% -> 2% of each run, Pallas kernels for 9% -> 12%
where the time goes in v3:
time: 125 us; the launch traced here: 124 us
  blocking collectives  49.4 us (40%)
  Pallas kernels  24.9 us (20%)
  waiting for transfers between devices  19.5 us (16%)
  between operations  14.2 us (11%)
  starting transfers between devices  12.4 us (10%)
  local copies, waits for them, and re-layouts  3.62 us (3%)
    all_to_all x1, blocking collectives, body(): by_z = lax.all_to_all(pairs, 'col', 0, 0, axis_index_groups=z_groups)  26.9 us
    pallas_call x6, Pallas kernels, call(): pl.pallas_call(kernel, out_shape=[jax.ShapeDtypeStruct(shape, dtype) for...  24.9 us
    all_to_all x1, blocking collectives, body(): gram = lax.all_to_all(gram, 'row', 0, 0).sum(axis=0)  22.5 us
    all_gather x1, waiting for transfers between devices, body(): diag = lax.all_gather(diag, 'row', axis=0)  10.1 us
    all_to_all x2, starting transfers between devices, spread(): lax.all_to_all(jnp.broadcast_to(block[None], (count,) + block.shape), axi...  8.32 us
    all_to_all x2, waiting for transfers between devices, spread(): lax.all_to_all(jnp.broadcast_to(block[None], (count,) + block.shape), axi...  6.31 us
    ppermute x1, starting transfers between devices, body(): share = lax.ppermute(share, ('row', 'col'), moves)  4.02 us
    ppermute x1, waiting for transfers between devices, body(): share = lax.ppermute(share, ('row', 'col'), moves)  3.04 us
  transfers between devices with their start and end apart: 5, of which 4 were waited for; matrix products, arithmetic and copies ran while one was open for 2% of the time, Pallas kernels for 12%

profile of v3, /device:TPU:1, one launch (start us, length us, event | category | flops | bytes accessed | tf_op | source)
XLA Modules:
  0.0 124.1 jit_solution(17701813162546890352)
XLA Ops:
  7.2 0.0 all-gather.5.cloned.1.call-start
  7.2 1.7 %shard_map.92 = (bf16[2,32,512]{2,1,0:T(8,128)(2,1)}, bf16[8,2,16,1024]{3,2,1,0:T(8,128)(2,1)}) custom-call(bf16[32,512]{1,0:T(8,128)(2,1)} %a_diag.1, bf16[32,512]{1,0:T(8,128)(2,1)} %linv_diag.1, bf16[16,1024]{1,0:T(8,128)(2,1)} %bitcast.12, bf16[16,1024]{1,0:T(8,128)(2,1)} %bitcast.13), custom_call_target="tpu_custom_call" | custom-call | flops 1048576 | bytes 2097 | tf_op jit(solution)/shard_map/pallas_call | solution.py:291
  8.9 0.0 all-gather.5.cloned.1.call-update
  9.0 26.9 %all_to_all.20 = bf16[8,2,16,1024]{3,2,1,0:T(8,128)(2,1)S(1)} all-to-all(bf16[8,2,16,1024]{3,2,1,0:T(8,128)(2,1)} %get-tuple-element.19), channel_id=1, replica_groups={{0,1,2,3,4,5,6,7},{8,9,10,11,12,13,14,15},{16,17,18,19,20,21,22,23},{24..., dimensions={0} | all-to-all | bytes 1048576 | tf_op jit(solution)/shard_map/all_to_all | solution.py:333
  35.8 1.6 %broadcast_in_dim.4 = bf16[4,8,2,16,1024]{4,3,2,1,0:T(8,128)(2,1)} broadcast(bf16[8,2,16,1024]{3,2,1,0:T(8,128)(2,1)S(1)} %all_to_all.20), dimensions={1,2,3,4} | broadcast | bytes 2621440 | tf_op jit(solution)/shard_map/broadcast_in_dim | solution.py:27
  37.4 4.5 %all-to-all-start.1 = ((bf16[4,8,2,16,1024]{4,3,2,1,0:T(8,128)(2,1)}), bf16[4,8,2,16,1024]{4,3,2,1,0:T(8,128)(2,1)}, u32[]{:S(2)}, u32[]{:S(2)}) async-start(bf16[4,8,2,16,1024]{4,3,2,1,0:T(8,128)(2,1)} %broadcast_in_dim.4), calls=%async_computation.1 | async-start | bytes 4194304 | tf_op jit(solution)/shard_map/all_to_all | solution.py:26
  41.9 0.0 all-gather.7.cloned.1.call-start
  42.0 4.0 %collective-permute-start = (bf16[2,2,16,512]{3,2,1,0:T(8,128)(2,1)S(1)}, bf16[2,2,16,512]{3,2,1,0:T(8,128)(2,1)S(1)}, u32[]{:S(2)}, u32[]{:S(2)}) collective-permute-start(bf16[2,2,16,512]{3,2,1,0:T(8,128)(2,1)S(1)} %constant_dynamic-slice_fusion), channel_id=1, source_target_pairs={{0,0},{1,32},{2,64},{3,96},{4,1},{5,33},{6,65},{7,97},{8,128},{9,1... | collective-permute-start | bytes 196616 | tf_op jit(solution)/shard_map/ppermute | solution.py:349
  46.0 3.0 %collective-permute-done = bf16[2,2,16,512]{3,2,1,0:T(8,128)(2,1)S(1)} collective-permute-done((bf16[2,2,16,512]{3,2,1,0:T(8,128)(2,1)S(1)}, bf16[2,2,16,512]{3,2,1,0:T(8,128)(2,1)S(1)}, u32[]{:S(2)}, u32[]{:S(2)}) %collective-permute-start) | collective-permute-done | bytes 65568 | tf_op jit(solution)/shard_map/ppermute | solution.py:349
  49.1 0.0 copy-start.1
  49.1 0.6 copy-done.1
  49.7 0.0 all-gather.7.cloned.1.call-update
  49.7 10.1 %all-gather.5.cloned.1.call-done = bf16[32,32,512]{2,1,0:T(8,128)(2,1)} async-done(((bf16[2,32,512]{2,1,0:T(8,128)(2,1)}), bf16[32,32,512]{2,1,0:T(8,128)(2,1)}) %all-gather.5.cloned.1.call-update) | async-done | bytes 1048592 | tf_op jit(solution)/shard_map/all_gather | solution.py:332
  59.8 3.5 %shard_map.93 = (bf16[16,32]{1,0:T(8,128)(2,1)}, bf16[512,512]{1,0:T(8,128)(2,1)}) custom-call(bf16[16,2,32,512]{3,2,1,0:T(8,128)(2,1)} %bitcast.8), custom_call_target="tpu_custom_call" | custom-call | flops 536870912 | bytes 1073741 | tf_op jit(solution)/shard_map/pallas_call | solution.py:291
  63.3 2.6 %all-to-all-done.1 = bf16[4,8,2,16,1024]{4,3,2,1,0:T(8,128)(2,1)} async-done(((bf16[4,8,2,16,1024]{4,3,2,1,0:T(8,128)(2,1)}), bf16[4,8,2,16,1024]{4,3,2,1,0:T(8,128)(2,1)}, u32[]{:S(2)}, u32[]{:S(2)}) %all-to-all-start.1) | async-done | bytes 2097184 | tf_op jit(solution)/shard_map/all_to_all | solution.py:26
  65.8 3.8 %shard_map.94 = (bf16[256,1024]{1,0:T(8,128)(2,1)}, bf16[256,1024]{1,0:T(8,128)(2,1)}, f32[16,8,256]{2,1,0:T(8,128)}) custom-call(bf16[16,2,32,512]{3,2,1,0:T(8,128)(2,1)} %bitcast.9, bf16[512,512]{1,0:T(8,128)(2,1)} %get-tuple-element.18.turned, bf16[32,2,16,1024]{3,2,1,0:T(8,128)(2,1)} %bitcast.3.rows), custom_call_target="tpu_custom_call" | custom-call | flops 536870912 | bytes 1073741 | tf_op jit(solution)/shard_map/pallas_call | solution.py:291
  69.7 22.5 %all_to_all.21 = f32[16,8,256]{2,1,0:T(8,128)S(1)} all-to-all(f32[16,8,256]{2,1,0:T(8,128)} %get-tuple-element.20), channel_id=1, replica_groups=mesh['row'=16,'col'=32] {'row'}, dimensions={0} | all-to-all | bytes 262144 | tf_op jit(solution)/shard_map/all_to_all | solution.py:417
  92.2 0.7 broadcast_in_dim.5
  92.9 3.9 %all-to-all-start.3 = ((f32[32,8,256]{2,1,0:T(8,128)}), f32[32,8,256]{2,1,0:T(8,128)S(1)}, u32[]{:S(2)}, u32[]{:S(2)}) async-start(f32[32,8,256]{2,1,0:T(8,128)} %broadcast_in_dim.5), calls=%async_computation.3 | async-start | bytes 524288 | tf_op jit(solution)/shard_map/all_to_all | solution.py:26
  96.8 2.6 %shard_map.96.l_rows = bf16[1024,512]{1,0:T(8,128)(2,1)} custom-call(bf16[32,2,16,1024]{3,2,1,0:T(8,128)(2,1)} %bitcast.3.rows), custom_call_target="tpu_custom_call" | custom-call | flops 524288000 | bytes 1048576 | tf_op jit(solution)/shard_map/pallas_call | solution.py:291
  99.3 4.5 %shard_map.95 = (bf16[1024,512]{1,0:T(8,128)(2,1)}, bf16[16,1024]{1,0:T(8,128)(2,1)}) custom-call(bf16[16,2,32,512]{3,2,1,0:T(8,128)(2,1)} %bitcast.10, bf16[512,512]{1,0:T(8,128)(2,1)} %get-tuple-element.18.turned, bf16[32,2,16,1024]{3,2,1,0:T(8,128)(2,1)} %bitcast.3.rows, bf16[256,1024]{1,0:T(8,128)(2,1)} %get-tuple-element.22.first, ...), custom_call_target="tpu_custom_call" | custom-call | flops 536870912 | bytes 1073741 | tf_op jit(solution)/shard_map/pallas_call | solution.py:291
  103.8 0.0 all-gather.7.cloned.1.call-done.cols
  103.9 3.8 %all-to-all-done.3.gram = f32[32,8,256]{2,1,0:T(8,128)S(1)} async-done(((f32[32,8,256]{2,1,0:T(8,128)}), f32[32,8,256]{2,1,0:T(8,128)S(1)}, u32[]{:S(2)}, u32[]{:S(2)}) %all-to-all-start.3) | async-done | bytes 262176 | tf_op jit(solution)/shard_map/all_to_all | solution.py:26
  107.6 0.0 copy-start
  107.6 0.7 copy-done
  108.3 8.9 %shard_map.97 = (f32[8,16]{1,0:T(8,128)}, f32[8,1024]{1,0:T(8,128)}, bf16[1024,512]{1,0:T(8,128)(2,1)}) custom-call(f32[32,8,256]{2,1,0:T(8,128)} %copy-done, bf16[256,1024]{1,0:T(8,128)(2,1)} %get-tuple-element.21.panel, bf16[16,2,32,512]{3,2,1,0:T(8,128)(2,1)} %bitcast.11, bf16[512,512]{1,0:T(8,128)(2,1)} %get-tuple-element.18.turned, ...), custom_call_target="tpu_custom_call" | custom-call | flops 1610612736 | bytes 3221225 | tf_op jit(solution)/shard_map/pallas_call | solution.py:291
  (2 shorter events, 0.0 us)
Async XLA Ops:
  7.2 52.7 %all-gather.5.cloned.1.call-start = ((), (), s32[]{:S(2)}) async-start(), calls=%async_computation.4 | async-start | bytes 1114112 | tf_op jit(solution)/shard_map/all_gather | solution.py:332
  37.4 28.4 %all-to-all-start.1 = ((bf16[4,8,2,16,1024]{4,3,2,1,0:T(8,128)(2,1)}), bf16[4,8,2,16,1024]{4,3,2,1,0:T(8,128)(2,1)}, u32[]{:S(2)}, u32[]{:S(2)}) async-start(bf16[4,8,2,16,1024]{4,3,2,1,0:T(8,128)(2,1)} %broadcast_in_dim.4), calls=%async_computation.1 | async-start | bytes 4194304 | tf_op jit(solution)/shard_map/all_to_all | solution.py:26
  41.9 62.0 %all-gather.7.cloned.1.call-start = ((), (), s32[]{:S(2)}) async-start(), calls=%async_computation.5 | async-start | bytes 1114112 | tf_op jit(solution)/shard_map/all_gather | solution.py:350
  42.0 7.1 %collective-permute-start = (bf16[2,2,16,512]{3,2,1,0:T(8,128)(2,1)S(1)}, bf16[2,2,16,512]{3,2,1,0:T(8,128)(2,1)S(1)}, u32[]{:S(2)}, u32[]{:S(2)}) collective-permute-start(bf16[2,2,16,512]{3,2,1,0:T(8,128)(2,1)S(1)} %constant_dynamic-slice_fusion), channel_id=1, source_target_pairs={{0,0},{1,32},{2,64},{3,96},{4,1},{5,33},{6,65},{7,97},{8,128},{9,1... | collective-permute-start | bytes 196616 | tf_op jit(solution)/shard_map/ppermute | solution.py:349
  49.1 0.6 copy-start.1
  92.9 14.7 %all-to-all-start.3 = ((f32[32,8,256]{2,1,0:T(8,128)}), f32[32,8,256]{2,1,0:T(8,128)S(1)}, u32[]{:S(2)}, u32[]{:S(2)}) async-start(f32[32,8,256]{2,1,0:T(8,128)} %broadcast_in_dim.5), calls=%async_computation.3 | async-start | bytes 524288 | tf_op jit(solution)/shard_map/all_to_all | solution.py:26
  107.6 0.7 copy-start
Sparse Core Ops, SparseCore 0:
  10.1 49.6 all-gather.4
  61.9 40.1 all-gather.6

commit v4 on v3

--- a/solution.py
+++ b/solution.py
@@ -77,16 +77,16 @@
     band = panel.shape[0]
     blocks, pieces = band // diag.shape[2], band // rows.shape[2]
     copies = start(
+        (diag.at[pl.ds(0, blocks), 1, :, pl.ds(0, band)], linv_in),
+        (rows.at[pl.ds(0, pieces), 0], a_in),
+        (turned.at[pl.ds(0, band)], c_in),
         (rows.at[:, 1], l_in),
-        (turned.at[pl.ds(0, band)], c_in),
-        (rows.at[pl.ds(0, pieces), 0], a_in),
-        (diag.at[pl.ds(0, blocks), 1, :, pl.ds(0, band)], linv_in),
         sem=sem,
     )
     wait(copies[:2])
+    solved = dot(linv_in[...].reshape(band, band), a_in[...].reshape(band, width), 1, 0)
+    wait(copies[2:])
     half = 0.5 * dot(c_in[...], l_in[...].reshape(order, width), 1, 0)
-    wait(copies[2:])
-    solved = dot(linv_in[...].reshape(band, band), a_in[...].reshape(band, width), 1, 0)
     f = (solved - half).astype(bf16)
     first_out[...] = f
     p = (f.astype(f32) - half).astype(bf16)

time: 125 us -> 125 us (level)
  transfers between devices with their start and end apart: 5 -> 5, of which waited for: 4 -> 4; matrix products, arithmetic and copies ran while one was open for 2% -> 2% of each run, Pallas kernels for 12% -> 11%
where the time goes in v4:
time: 125 us; the launch traced here: 123 us
  blocking collectives  49.3 us (39%)
  Pallas kernels  24.8 us (20%)
  waiting for transfers between devices  19.1 us (15%)
  between operations  14.2 us (11%)
  starting transfers between devices  12.4 us (10%)
  local copies, waits for them, and re-layouts  3.62 us (3%)
    all_to_all x1, blocking collectives, body(): by_z = lax.all_to_all(pairs, 'col', 0, 0, axis_index_groups=z_groups)  26.9 us
    pallas_call x6, Pallas kernels, call(): pl.pallas_call(kernel, out_shape=[jax.ShapeDtypeStruct(shape, dtype) for...  24.8 us
    all_to_all x1, blocking collectives, body(): gram = lax.all_to_all(gram, 'row', 0, 0).sum(axis=0)  22.5 us
    all_gather x1, waiting for transfers between devices, body(): diag = lax.all_gather(diag, 'row', axis=0)  10.1 us
    all_to_all x2, starting transfers between devices, spread(): lax.all_to_all(jnp.broadcast_to(block[None], (count,) + block.shape), axi...  8.32 us
    all_to_all x2, waiting for transfers between devices, spread(): lax.all_to_all(jnp.broadcast_to(block[None], (count,) + block.shape), axi...  5.93 us
    ppermute x1, starting transfers between devices, body(): share = lax.ppermute(share, ('row', 'col'), moves)  4.02 us
    ppermute x1, waiting for transfers between devices, body(): share = lax.ppermute(share, ('row', 'col'), moves)  3.04 us
  transfers between devices with their start and end apart: 5, of which 4 were waited for; matrix products, arithmetic and copies ran while one was open for 2% of the time, Pallas kernels for 11%

profile of v4, /device:TPU:1, one launch (start us, length us, event | category | flops | bytes accessed | tf_op | source)
XLA Modules:
  0.0 123.5 jit_solution(2631233072416751095)
XLA Ops:
  7.2 0.0 all-gather.5.cloned.1.call-start
  7.2 1.7 %shard_map.92 = (bf16[2,32,512]{2,1,0:T(8,128)(2,1)}, bf16[8,2,16,1024]{3,2,1,0:T(8,128)(2,1)}) custom-call(bf16[32,512]{1,0:T(8,128)(2,1)} %a_diag.1, bf16[32,512]{1,0:T(8,128)(2,1)} %linv_diag.1, bf16[16,1024]{1,0:T(8,128)(2,1)} %bitcast.12, bf16[16,1024]{1,0:T(8,128)(2,1)} %bitcast.13), custom_call_target="tpu_custom_call" | custom-call | flops 1048576 | bytes 2097 | tf_op jit(solution)/shard_map/pallas_call | solution.py:291
  8.9 0.0 all-gather.5.cloned.1.call-update
  9.0 26.9 %all_to_all.20 = bf16[8,2,16,1024]{3,2,1,0:T(8,128)(2,1)S(1)} all-to-all(bf16[8,2,16,1024]{3,2,1,0:T(8,128)(2,1)} %get-tuple-element.19), channel_id=1, replica_groups={{0,1,2,3,4,5,6,7},{8,9,10,11,12,13,14,15},{16,17,18,19,20,21,22,23},{24..., dimensions={0} | all-to-all | bytes 1048576 | tf_op jit(solution)/shard_map/all_to_all | solution.py:333
  35.8 1.6 %broadcast_in_dim.4 = bf16[4,8,2,16,1024]{4,3,2,1,0:T(8,128)(2,1)} broadcast(bf16[8,2,16,1024]{3,2,1,0:T(8,128)(2,1)S(1)} %all_to_all.20), dimensions={1,2,3,4} | broadcast | bytes 2621440 | tf_op jit(solution)/shard_map/broadcast_in_dim | solution.py:27
  37.4 4.5 %all-to-all-start.1 = ((bf16[4,8,2,16,1024]{4,3,2,1,0:T(8,128)(2,1)}), bf16[4,8,2,16,1024]{4,3,2,1,0:T(8,128)(2,1)}, u32[]{:S(2)}, u32[]{:S(2)}) async-start(bf16[4,8,2,16,1024]{4,3,2,1,0:T(8,128)(2,1)} %broadcast_in_dim.4), calls=%async_computation.1 | async-start | bytes 4194304 | tf_op jit(solution)/shard_map/all_to_all | solution.py:26
  41.9 0.0 all-gather.7.cloned.1.call-start
  42.0 4.0 %collective-permute-start = (bf16[2,2,16,512]{3,2,1,0:T(8,128)(2,1)S(1)}, bf16[2,2,16,512]{3,2,1,0:T(8,128)(2,1)S(1)}, u32[]{:S(2)}, u32[]{:S(2)}) collective-permute-start(bf16[2,2,16,512]{3,2,1,0:T(8,128)(2,1)S(1)} %constant_dynamic-slice_fusion), channel_id=1, source_target_pairs={{0,0},{1,32},{2,64},{3,96},{4,1},{5,33},{6,65},{7,97},{8,128},{9,1... | collective-permute-start | bytes 196616 | tf_op jit(solution)/shard_map/ppermute | solution.py:349
  46.0 3.0 %collective-permute-done = bf16[2,2,16,512]{3,2,1,0:T(8,128)(2,1)S(1)} collective-permute-done((bf16[2,2,16,512]{3,2,1,0:T(8,128)(2,1)S(1)}, bf16[2,2,16,512]{3,2,1,0:T(8,128)(2,1)S(1)}, u32[]{:S(2)}, u32[]{:S(2)}) %collective-permute-start) | collective-permute-done | bytes 65568 | tf_op jit(solution)/shard_map/ppermute | solution.py:349
  49.1 0.0 copy-start.1
  49.1 0.6 copy-done.1
  49.7 0.0 all-gather.7.cloned.1.call-update
  49.7 10.1 %all-gather.5.cloned.1.call-done = bf16[32,32,512]{2,1,0:T(8,128)(2,1)} async-done(((bf16[2,32,512]{2,1,0:T(8,128)(2,1)}), bf16[32,32,512]{2,1,0:T(8,128)(2,1)}) %all-gather.5.cloned.1.call-update) | async-done | bytes 1048592 | tf_op jit(solution)/shard_map/all_gather | solution.py:332
  59.8 3.5 %shard_map.93 = (bf16[16,32]{1,0:T(8,128)(2,1)}, bf16[512,512]{1,0:T(8,128)(2,1)}) custom-call(bf16[16,2,32,512]{3,2,1,0:T(8,128)(2,1)} %bitcast.8), custom_call_target="tpu_custom_call" | custom-call | flops 536870912 | bytes 1073741 | tf_op jit(solution)/shard_map/pallas_call | solution.py:291
  63.3 2.6 %all-to-all-done.1 = bf16[4,8,2,16,1024]{4,3,2,1,0:T(8,128)(2,1)} async-done(((bf16[4,8,2,16,1024]{4,3,2,1,0:T(8,128)(2,1)}), bf16[4,8,2,16,1024]{4,3,2,1,0:T(8,128)(2,1)}, u32[]{:S(2)}, u32[]{:S(2)}) %all-to-all-start.1) | async-done | bytes 2097184 | tf_op jit(solution)/shard_map/all_to_all | solution.py:26
  65.8 3.7 %shard_map.94 = (bf16[256,1024]{1,0:T(8,128)(2,1)}, bf16[256,1024]{1,0:T(8,128)(2,1)}, f32[16,8,256]{2,1,0:T(8,128)}) custom-call(bf16[16,2,32,512]{3,2,1,0:T(8,128)(2,1)} %bitcast.9, bf16[512,512]{1,0:T(8,128)(2,1)} %get-tuple-element.18.turned, bf16[32,2,16,1024]{3,2,1,0:T(8,128)(2,1)} %bitcast.3.rows), custom_call_target="tpu_custom_call" | custom-call | flops 536870912 | bytes 1073741 | tf_op jit(solution)/shard_map/pallas_call | solution.py:291
  69.5 22.5 %all_to_all.21 = f32[16,8,256]{2,1,0:T(8,128)S(1)} all-to-all(f32[16,8,256]{2,1,0:T(8,128)} %get-tuple-element.20), channel_id=1, replica_groups=mesh['row'=16,'col'=32] {'row'}, dimensions={0} | all-to-all | bytes 262144 | tf_op jit(solution)/shard_map/all_to_all | solution.py:417
  92.0 0.7 broadcast_in_dim.5
  92.7 3.9 %all-to-all-start.3 = ((f32[32,8,256]{2,1,0:T(8,128)}), f32[32,8,256]{2,1,0:T(8,128)S(1)}, u32[]{:S(2)}, u32[]{:S(2)}) async-start(f32[32,8,256]{2,1,0:T(8,128)} %broadcast_in_dim.5), calls=%async_computation.3 | async-start | bytes 524288 | tf_op jit(solution)/shard_map/all_to_all | solution.py:26
  96.6 2.6 %shard_map.96.l_rows = bf16[1024,512]{1,0:T(8,128)(2,1)} custom-call(bf16[32,2,16,1024]{3,2,1,0:T(8,128)(2,1)} %bitcast.3.rows), custom_call_target="tpu_custom_call" | custom-call | flops 524288000 | bytes 1048576 | tf_op jit(solution)/shard_map/pallas_call | solution.py:291
  99.1 4.5 %shard_map.95 = (bf16[1024,512]{1,0:T(8,128)(2,1)}, bf16[16,1024]{1,0:T(8,128)(2,1)}) custom-call(bf16[16,2,32,512]{3,2,1,0:T(8,128)(2,1)} %bitcast.10, bf16[512,512]{1,0:T(8,128)(2,1)} %get-tuple-element.18.turned, bf16[32,2,16,1024]{3,2,1,0:T(8,128)(2,1)} %bitcast.3.rows, bf16[256,1024]{1,0:T(8,128)(2,1)} %get-tuple-element.22.first, ...), custom_call_target="tpu_custom_call" | custom-call | flops 536870912 | bytes 1073741 | tf_op jit(solution)/shard_map/pallas_call | solution.py:291
  103.6 0.0 all-gather.7.cloned.1.call-done.cols
  103.7 3.4 %all-to-all-done.3.gram = f32[32,8,256]{2,1,0:T(8,128)S(1)} async-done(((f32[32,8,256]{2,1,0:T(8,128)}), f32[32,8,256]{2,1,0:T(8,128)S(1)}, u32[]{:S(2)}, u32[]{:S(2)}) %all-to-all-start.3) | async-done | bytes 262176 | tf_op jit(solution)/shard_map/all_to_all | solution.py:26
  107.0 0.0 copy-start
  107.0 0.7 copy-done
  107.7 8.9 %shard_map.97 = (f32[8,16]{1,0:T(8,128)}, f32[8,1024]{1,0:T(8,128)}, bf16[1024,512]{1,0:T(8,128)(2,1)}) custom-call(f32[32,8,256]{2,1,0:T(8,128)} %copy-done, bf16[256,1024]{1,0:T(8,128)(2,1)} %get-tuple-element.21.panel, bf16[16,2,32,512]{3,2,1,0:T(8,128)(2,1)} %bitcast.11, bf16[512,512]{1,0:T(8,128)(2,1)} %get-tuple-element.18.turned, ...), custom_call_target="tpu_custom_call" | custom-call | flops 1610612736 | bytes 3221225 | tf_op jit(solution)/shard_map/pallas_call | solution.py:291
  (2 shorter events, 0.0 us)
Async XLA Ops:
  7.2 52.7 %all-gather.5.cloned.1.call-start = ((), (), s32[]{:S(2)}) async-start(), calls=%async_computation.4 | async-start | bytes 1114112 | tf_op jit(solution)/shard_map/all_gather | solution.py:332
  37.4 28.4 %all-to-all-start.1 = ((bf16[4,8,2,16,1024]{4,3,2,1,0:T(8,128)(2,1)}), bf16[4,8,2,16,1024]{4,3,2,1,0:T(8,128)(2,1)}, u32[]{:S(2)}, u32[]{:S(2)}) async-start(bf16[4,8,2,16,1024]{4,3,2,1,0:T(8,128)(2,1)} %broadcast_in_dim.4), calls=%async_computation.1 | async-start | bytes 4194304 | tf_op jit(solution)/shard_map/all_to_all | solution.py:26
  41.9 61.8 %all-gather.7.cloned.1.call-start = ((), (), s32[]{:S(2)}) async-start(), calls=%async_computation.5 | async-start | bytes 1114112 | tf_op jit(solution)/shard_map/all_gather | solution.py:350
  42.0 7.1 %collective-permute-start = (bf16[2,2,16,512]{3,2,1,0:T(8,128)(2,1)S(1)}, bf16[2,2,16,512]{3,2,1,0:T(8,128)(2,1)S(1)}, u32[]{:S(2)}, u32[]{:S(2)}) collective-permute-start(bf16[2,2,16,512]{3,2,1,0:T(8,128)(2,1)S(1)} %constant_dynamic-slice_fusion), channel_id=1, source_target_pairs={{0,0},{1,32},{2,64},{3,96},{4,1},{5,33},{6,65},{7,97},{8,128},{9,1... | collective-permute-start | bytes 196616 | tf_op jit(solution)/shard_map/ppermute | solution.py:349
  49.1 0.6 copy-start.1
  92.7 14.3 %all-to-all-start.3 = ((f32[32,8,256]{2,1,0:T(8,128)}), f32[32,8,256]{2,1,0:T(8,128)S(1)}, u32[]{:S(2)}, u32[]{:S(2)}) async-start(f32[32,8,256]{2,1,0:T(8,128)} %broadcast_in_dim.5), calls=%async_computation.3 | async-start | bytes 524288 | tf_op jit(solution)/shard_map/all_to_all | solution.py:26
  107.0 0.7 copy-start
Sparse Core Ops, SparseCore 0:
  10.1 49.6 all-gather.4
  61.9 40.1 all-gather.6
